TPU v7x, 256 devices: a whole 4x4x8 slice. The times are simulated.
256 devices in a mesh: seq: 32 (over x, z), head: 8 (over y, core).
Axes of the slice: x: 4, y: 4, z: 8, core: 2. Of those that a mesh axis runs over, the one named last changes fastest.
Arguments:
- queries: bfloat16 [65536, 4096], P('seq', 'head'), may hold values from -64 to 64
- keys: bfloat16 [65536, 1024], P('seq', 'head'), may hold values from -13 to 13
- values: bfloat16 [65536, 1024], P('seq', 'head'), may hold values from -18 to 18
- assignments: int32 [8, 65536], P('head', 'seq'), may hold values from 0 to 511, as said below
- norm_gain: float32 [4096], P('head'), may hold values from 0.5 to 1.5
Outputs:
- normed: bfloat16 [65536, 4096], P('seq', 'head')
Inputs may be any that keep to these rules, and one draw needn't show every extreme that they name: `assignments`: every code is assigned to one or more tokens of each key head.
All inputs are finite; a program needn't handle non-finite values.
Results may differ from a plain program's by a relative error of at most 0.0074.
Values may be sent and summed in bfloat16 or wider, within the bound.
No kernel may reach another device: no remote copies, remote signals or barrier semaphores. Data moves between devices by JAX's collectives and lax.ppermute only.
A program may use at most 128 MiB of HBM per device.

v0:
```python
import math

import jax
import jax.numpy as jnp
from jax import lax
from jax.sharding import PartitionSpec as P

DH = 128
QH = 32
CODES = 512
BLK = 256


def carried_in(shard, axis, combine, identity):
    peers, here = (lax.axis_size(axis), lax.axis_index(axis))
    everything = jax.tree.map(lambda part: lax.all_gather(part, axis), shard)
    start = jax.tree.map(
        lambda part, zero: jnp.broadcast_to(jnp.asarray(zero, part.dtype), part.shape),
        shard,
        identity,
    )

    def turn(k, before):
        reached = k < here
        new = combine(before, jax.tree.map(lambda part: part[k], everything))
        return jax.tree.map(lambda a, b: jnp.where(reached, a, b), new, before)

    return lax.fori_loop(0, peers, turn, start)


def from_behind(shard, axis, by):
    peers = lax.axis_size(axis)
    pairs = [(i, i + by) for i in range(peers) if 0 <= i + by < peers]
    return lax.ppermute(shard, axis, pairs)


def attend_block(
    query_rows,
    cur_keys,
    cur_values,
    prev_keys,
    prev_values,
    cache_values,
    cache_counts,
    codes,
    has_prev,
):
    scale = 1.0 / math.sqrt(DH)
    code_scores = (
        jnp.einsum("thgd,hcd->hgtc", query_rows, codes, preferred_element_type=jnp.float32) * scale
    )
    prev_scores = (
        jnp.einsum("thgd,hjd->hgtj", query_rows, prev_keys, preferred_element_type=jnp.float32)
        * scale
    )
    cur_scores = (
        jnp.einsum("thgd,hjd->hgtj", query_rows, cur_keys, preferred_element_type=jnp.float32)
        * scale
    )
    width = cur_keys.shape[1]
    causal = (
        jnp.arange(width, dtype=jnp.int32)[:, None] >= jnp.arange(width, dtype=jnp.int32)[None, :]
    )
    valid = (cache_counts > 0.0)[:, None, None, :]
    lowest = jnp.asarray(-jnp.inf, jnp.float32)
    top = jnp.maximum(
        jnp.max(jnp.where(valid, code_scores, lowest), axis=-1),
        jnp.max(jnp.where(causal, cur_scores, lowest), axis=-1),
    )
    top = jnp.maximum(top, jnp.where(has_prev > 0.0, jnp.max(prev_scores, axis=-1), lowest))
    code_weights = jnp.where(valid, jnp.exp(code_scores - top[..., None]), 0.0)
    prev_weights = jnp.exp(prev_scores - top[..., None]) * has_prev
    cur_weights = jnp.where(causal, jnp.exp(cur_scores - top[..., None]), 0.0)
    denominator = (
        jnp.sum(code_weights * cache_counts[:, None, None, :], axis=-1)
        + jnp.sum(prev_weights, axis=-1)
        + jnp.sum(cur_weights, axis=-1)
    )
    numerator = jnp.einsum(
        "hgtc,hcd->thgd",
        code_weights.astype(jnp.bfloat16),
        cache_values,
        preferred_element_type=jnp.float32,
    )
    numerator = numerator + jnp.einsum(
        "hgtj,jhd->thgd",
        prev_weights.astype(jnp.bfloat16),
        prev_values,
        preferred_element_type=jnp.float32,
    )
    numerator = numerator + jnp.einsum(
        "hgtj,jhd->thgd",
        cur_weights.astype(jnp.bfloat16),
        cur_values,
        preferred_element_type=jnp.float32,
    )
    attended = numerator / jnp.transpose(denominator, (2, 0, 1))[..., None]
    return attended.reshape(attended.shape[0], -1)


def combine_totals(earlier, later):
    present = later[4] > 0.0
    front_sums = jnp.where(present, earlier[0] + earlier[1] + later[0], earlier[0])
    tail_sums = jnp.where(present, later[1], earlier[1])
    front_counts = jnp.where(present, earlier[2] + earlier[3] + later[2], earlier[2])
    tail_counts = jnp.where(present, later[3], earlier[3])
    return (front_sums, tail_sums, front_counts, tail_counts, jnp.maximum(earlier[4], later[4]))


def local(queries, keys, values, assignments, norm_gain):
    kv_heads = assignments.shape[0]
    tok_rows = assignments.shape[1]
    head_dim = keys.shape[1] // kv_heads
    group_size = queries.shape[1] // keys.shape[1]
    num_blocks = tok_rows // BLK
    code_ids = jnp.arange(CODES, dtype=jnp.int32)
    member = (assignments[:, :, None] == code_ids[None, None, :]).astype(jnp.bfloat16)
    key_heads = keys.reshape(tok_rows, kv_heads, head_dim)
    value_heads = values.reshape(tok_rows, kv_heads, head_dim)
    key_sums = jnp.einsum("htc,thd->hcd", member, key_heads, preferred_element_type=jnp.float32)
    code_counts = jnp.sum(member, axis=1, dtype=jnp.float32)
    block_member = member.reshape(kv_heads, num_blocks, BLK, CODES)
    value_blocks = value_heads.reshape(num_blocks, BLK, kv_heads, head_dim)
    block_sums = jnp.einsum(
        "hbtc,bthd->hbcd", block_member, value_blocks, preferred_element_type=jnp.float32
    )
    block_counts = jnp.sum(block_member, axis=2, dtype=jnp.float32)
    front_sums = jnp.sum(block_sums[:, : num_blocks - 1], axis=1)
    front_counts = jnp.sum(block_counts[:, : num_blocks - 1], axis=1)
    tail_sums = block_sums[:, num_blocks - 1]
    tail_counts = block_counts[:, num_blocks - 1]
    total_sums, total_counts = lax.psum((key_sums, code_counts), "seq")
    codes = (total_sums / total_counts[:, :, None]).astype(jnp.bfloat16)
    zero_sums = jnp.zeros_like(front_sums)
    zero_counts = jnp.zeros_like(front_counts)
    present_flag = jnp.ones((1,), jnp.float32)
    empty_flag = jnp.zeros((1,), jnp.float32)
    before_sums, last_sums, before_counts, last_counts, seen_flag = carried_in(
        (front_sums, tail_sums, front_counts, tail_counts, present_flag),
        "seq",
        combine_totals,
        (zero_sums, zero_sums, zero_counts, zero_counts, empty_flag),
    )
    quantized = jax.vmap(lambda table, picks: jnp.take(table, picks, axis=0))(codes, assignments)
    received_keys, received_values = from_behind(
        (quantized[:, tok_rows - BLK :], value_heads[tok_rows - BLK :]), "seq", 1
    )
    key_blocks = quantized.reshape(kv_heads, num_blocks, BLK, head_dim).transpose(1, 0, 2, 3)
    prev_key_blocks = jnp.concatenate([received_keys[None], key_blocks[: num_blocks - 1]], axis=0)
    prev_value_blocks = jnp.concatenate(
        [received_values[None], value_blocks[: num_blocks - 1]], axis=0
    )
    first_flag = (lax.axis_index("seq") > 0).astype(jnp.float32)
    prev_flags = jnp.concatenate([first_flag[None], jnp.ones((num_blocks - 1,), jnp.float32)])
    running_sums = jnp.cumsum(block_sums, axis=1)
    running_counts = jnp.cumsum(block_counts, axis=1)
    earlier_sums = jnp.concatenate(
        [jnp.zeros_like(block_sums[:, :1]), running_sums[:, : num_blocks - 1]], axis=1
    )
    earlier_counts = jnp.concatenate(
        [jnp.zeros_like(block_counts[:, :1]), running_counts[:, : num_blocks - 1]], axis=1
    )
    base_sums = before_sums + last_sums
    base_counts = before_counts + last_counts
    cache_sums = jnp.concatenate(
        [before_sums[:, None], base_sums[:, None] + earlier_sums[:, : num_blocks - 1]], axis=1
    )
    cache_counts = jnp.concatenate(
        [before_counts[:, None], base_counts[:, None] + earlier_counts[:, : num_blocks - 1]], axis=1
    )
    cache_values = cache_sums.astype(jnp.bfloat16).transpose(1, 0, 2, 3)
    cache_counts = cache_counts.transpose(1, 0, 2)
    query_blocks = queries.reshape(num_blocks, BLK, kv_heads, group_size, head_dim)

    def per_block(inputs):
        (
            query_rows,
            cur_keys,
            cur_values,
            prev_keys,
            prev_values,
            block_cache,
            block_cache_counts,
            has_prev,
        ) = inputs
        return attend_block(
            query_rows,
            cur_keys,
            cur_values,
            prev_keys,
            prev_values,
            block_cache,
            block_cache_counts,
            codes,
            has_prev,
        )

    attended = lax.map(
        per_block,
        (
            query_blocks,
            key_blocks,
            value_blocks,
            prev_key_blocks,
            prev_value_blocks,
            cache_values,
            cache_counts,
            prev_flags,
        ),
    )
    attended = attended.reshape(tok_rows, queries.shape[1])
    partial_squares = jnp.sum(attended * attended, axis=1)
    total_squares = lax.psum(partial_squares, "head")
    mean_square = total_squares / (QH * DH)
    return (attended * lax.rsqrt(mean_square + 1e-06)[:, None] * norm_gain).astype(jnp.bfloat16)


def solution(mesh):
    in_specs = (P("seq", "head"), P("seq", "head"), P("seq", "head"), P("head", "seq"), P("head"))
    out_specs = P("seq", "head")
    return jax.shard_map(local, mesh=mesh, in_specs=in_specs, out_specs=out_specs, check_vma=False)
```

profile of v0, /device:TPU:1, one launch (start us, length us, event | category | flops | bytes accessed | tf_op | source)
XLA Modules:
  0.0 660.4 jit_solution(8658526188679667330)
XLA Ops:
  7.6 3.0 fusion.61
  14.3 4.4 collective-permute-start.1
  23.8 4.0 reshape.412
  29.7 61.8 %all-reduce.4 = (f32[32]{0:T(128)}, f32[512]{0:T(512)}) all-reduce(f32[32]{0:T(128)S(1)} %dynamic-update-slice, f32[512]{0:T(512)S(1)} %convert_reduce_fusion), channel_id=1, replica_groups=mesh['seq'=32,'head'=8] {'seq'}, use_global_device_ids=true, to_apply=%add.3 | all-reduce | flops 544 | bytes 4352
  91.5 37.4 %all-gather.2 = f32[32,1,512]{2,1,0:T(1,128)} all-gather(f32[1,1,512]{2,1,0:T(1,128)S(1)} %bitcast.237), channel_id=3, replica_groups=mesh['seq'=32,'head'=8] {'seq'}, dimensions={0}, use_global_device_ids=true | all-gather | bytes 67584 | tf_op jit(solution)/shard_map/all_gather | solution.py:16
  128.9 40.4 %all_gather.27 = f32[32,1,512]{2,1,0:T(1,128)} all-gather(f32[1,1,512]{2,1,0:T(1,128)S(1)} %slice.65), channel_id=1, replica_groups=mesh['seq'=32,'head'=8] {'seq'}, dimensions={0}, use_global_device_ids=true | all-gather | bytes 67584 | tf_op jit(solution)/shard_map/all_gather | solution.py:16
  171.9 8.6 %gather_fusion = bf16[2048,128]{1,0:T(8,128)(2,1)S(1)} fusion(bf16[1,512,128]{2,1,0:T(8,128)(2,1)S(1)} %divide_convert_fusion, s32[2048]{0:T(1024)S(1)} %bitcast.215), kind=kCustom, calls=%fused_computation | custom fusion | bytes 1064960 | tf_op jit(solution)/shard_map/vmap(jit(_take))/gather | solution.py:144
  181.5 2.7 collective-permute-start
  186.1 70.0 %all-gather.6.cloned.1.call-done = f32[32,1,512,128]{3,2,1,0:T(8,128)} async-done(((f32[1,1,512,128]{3,2,1,0:T(8,128)}), f32[32,1,512,128]{3,2,1,0:T(8,128)}) %all-gather.6.cloned.1.call-update) | async-done | bytes 8388624 | tf_op jit(solution)/shard_map/all_gather | solution.py:16
  256.1 98.0 %all-gather.8.cloned.1.call-done = f32[16384,128]{1,0:T(8,128)} async-done(((f32[512,128]{1,0:T(8,128)}), f32[16384,128]{1,0:T(8,128)}) %all-gather.8.cloned.1.call-update) | async-done | bytes 8388624 | tf_op jit(solution)/shard_map/all_gather | solution.py:16
  354.1 149.7 %while.31 = (s32[]{:T(128)}, f32[1,512,128]{2,1,0:T(8,128)S(1)}, f32[1,512,128]{2,1,0:T(8,128)S(1)}, f32[1,512]{1,0:T(1,128)S(1)}, f32[1,512]{1,0:T(1,128)S(1)},...) while((s32[]{:T(128)}, f32[1,512,128]{2,1,0:T(8,128)S(1)}, ...), condition=%wide.region_7.8_spmd.clone, body=%wide.region_6.7_spmd.clone.sunk | while | flops 528389 | bytes 1585318 | solution.py:28
  355.4 2.0 select_select_fusion.3
  360.1 2.0 select_select_fusion.3
  364.7 2.0 select_select_fusion.3
  369.4 2.0 select_select_fusion.3
  374.1 2.0 select_select_fusion.3
  383.4 2.0 select_select_fusion.3
  397.5 2.0 select_select_fusion.3
  402.2 2.0 select_select_fusion.3
  506.4 122.5 %while.30 = (s32[]{:T(128)}, f32[8,256,512]{1,2,0:T(8,128)}, bf16[8,1,512,128]{3,2,0,1:T(8,128)(2,1)}, f32[8,1,512]{2,0,1:T(8,128)}, bf16[8,256,1,4,128]{4,3,1,0...) while((s32[]{:T(128)}, f32[8,256,512]{1,2,0:T(8,128)}, ...), condition=%wide.region_17.18_spmd, body=%wide.region_10.17_spmd.sunk | while | flops 548077056 | bytes 26834112 | solution.py:198
  512.8 2.2 multiply_reduce_fusion.3
  528.1 2.2 multiply_reduce_fusion.3
  543.4 2.2 multiply_reduce_fusion.3
  558.7 2.2 multiply_reduce_fusion.3
  574.1 2.2 multiply_reduce_fusion.3
  589.4 2.2 multiply_reduce_fusion.3
  604.7 2.2 multiply_reduce_fusion.3
  620.0 2.2 multiply_reduce_fusion.3
  629.0 5.3 copy.46
  634.3 2.5 multiply_reduce_fusion.1
  636.8 13.1 %psum.23 = f32[2048]{0:T(1024)S(1)} all-reduce(f32[2048]{0:T(1024)S(1)} %bitcast.235), channel_id=1, replica_groups=mesh['seq'=32,'head'=8] {'head'}, use_global_device_ids=true, to_apply=%region_19.20 | all-reduce | flops 2048 | bytes 16384 | tf_op jit(solution)/shard_map/psum | solution.py:213
  649.9 3.9 fusion.51
  (292 shorter events, 251.8 us)
Async XLA Ops:
  6.5 1.0 copy-start
  6.5 4.6 copy-start.4
  6.5 5.3 copy-start.2
  6.5 164.2 %all-reduce.7.cloned.1.call-start = ((), (), s32[]{:S(2)}) async-start(), calls=%async_computation.1 | async-start | bytes 524288 | tf_op jit(solution)/shard_map/psum | solution.py:132
  10.6 245.5 %all-gather.6.cloned.1.call-start = ((), (), s32[]{:S(2)}) async-start(), calls=%async_computation | async-start | bytes 8650752 | tf_op jit(solution)/shard_map/all_gather | solution.py:16
  13.4 340.7 %all-gather.8.cloned.1.call-start = ((), (), s32[]{:S(2)}) async-start(), calls=%async_computation.2 | async-start | bytes 8650752 | tf_op jit(solution)/shard_map/all_gather | solution.py:16
  14.3 155.6 %collective-permute-start.1 = (bf16[256,1,128]{2,0,1:T(8,128)(2,1)S(1)}, bf16[256,1,128]{2,0,1:T(8,128)(2,1)S(1)}, u32[]{:S(2)}, u32[]{:S(2)}) collective-permute-start(bf16[256,1,128]{2,0,1:T(8,128)(2,1)S(1)} %slice_bitcast_fusion), channel_id=1, source_target_pairs={{0,8},{8,16},{16,24},{24,32},{32,40},{40,48},{48,56},{56,64},{64,7... | collective-permute-start | bytes 196616 | tf_op jit(solution)/shard_map/ppermute | solution.py:34
  23.2 4.6 copy-start.5
  23.8 4.0 copy-start.7
  23.8 146.1 %copy-start.3 = (bf16[1792,128]{1,0:T(8,128)(2,1)S(1)}, bf16[1792,128]{1,0:T(8,128)(2,1)}, u32[]{:S(2)}) copy-start(bf16[1792,128]{1,0:T(8,128)(2,1)} %slice.58) | copy-start | bytes 1376260
  181.5 4.6 collective-permute-start
  505.1 1.3 copy-start.8
  516.1 3.2 copy-start.1
  531.4 3.2 copy-start.1
  546.7 3.2 copy-start.1
  562.0 3.2 copy-start.1
  577.4 3.2 copy-start.1
  592.7 3.2 copy-start.1
  608.0 3.2 copy-start.1
  623.3 3.2 copy-start.1
  634.3 15.6 %copy-start.6 = (f32[512]{0:T(512)S(1)}, f32[512]{0:T(512)}, u32[]{:S(2)}) copy-start(f32[512]{0:T(512)} %param.13) | copy-start | bytes 6148
Sparse Core Ops, SparseCore 0:
  10.8 143.3 all-reduce.6
  156.8 99.2 all-gather.5
  258.7 95.3 all-gather.7
where the time goes:
time: 666 us; the launch traced here: 660 us
  other arithmetic  195 us (29%)
  waiting for transfers between devices  168 us (25%)
  blocking collectives  153 us (23%)
  matrix products  67.9 us (10%)
  local copies, waits for them, and re-layouts  50.3 us (8%)
  between operations  13.4 us (2%)
  starting transfers between devices  7.12 us (1%)
    all_gather x2, waiting for transfers between devices, carried_in(): everything = jax.tree.map(lambda part: lax.all_gather(part, axis), shard)  168 us
    select_n x64, other arithmetic, turn(): return jax.tree.map(lambda a, b: jnp.where(reached, a, b), new, before)  108 us
    all_gather x2, blocking collectives, carried_in(): everything = jax.tree.map(lambda part: lax.all_gather(part, axis), shard)  77.8 us
    unnamed x1, blocking collectives  61.8 us
    gt x32, other arithmetic, combine_totals(): present = later[4] > 0.0  41.5 us
    dynamic_slice x24, local copies, waits for them, and re-layouts, local(): lax.map(per_block, (query_blocks, key_blocks, value_blocks, prev_key_bloc...  19.4 us
    reduce_sum x8, other arithmetic, attend_block(): jnp.sum(code_weights * cache_counts[:, None, None, :], axis=-1)  18 us
    dot_general x8, matrix products, attend_block(): jnp.einsum('hgtj,jhd->thgd', prev_weights.astype(jnp.bfloat16), prev_valu...  15.7 us
  transfers between devices with their start and end apart: 5, of which 2 were waited for; matrix products, arithmetic and copies ran while one was open for 4% of the time, Pallas kernels for 0%

commit v1 on v0

v1 whole, which is shorter than its diff:
```python
import functools
import math

import jax
import jax.numpy as jnp
from jax import lax
from jax.experimental import pallas as pl
from jax.experimental.pallas import tpu as pltpu
from jax.sharding import PartitionSpec as P

DH = 128
CODES = 512
CHUNK = 128
MASKED = -1e30
F32 = jnp.float32
BF16 = jnp.bfloat16
KEEP = 1.0 / math.sqrt(DH) * math.log2(math.e)


def one_hot(picks, rows, first=0):
    ids = lax.broadcasted_iota(jnp.int32, (rows, picks.shape[1]), 0) + first
    return jnp.where(ids == picks, 1.0, 0.0).astype(BF16)


def high_low(x):
    high = x.astype(BF16)
    return high, (x - high.astype(F32)).astype(BF16)


def sums_kernel(peers, picks_ref, keys_ref, values_ref, out_ref, seen_ref, member, both):
    tokens = keys_ref.shape[0]
    share = CODES // peers
    both[:, :DH] = keys_ref[...]
    both[:, DH:] = values_ref[...]
    for t in range(0, tokens, 512):
        member[:, t : t + 512] = one_hot(picks_ref[:, t : t + 512], CODES)
    sums = jnp.dot(member[...], both[...], preferred_element_type=F32)
    rows = lax.broadcasted_iota(jnp.int32, (seen_ref.shape[0], tokens), 0)
    cols = lax.broadcasted_iota(jnp.int32, (seen_ref.shape[0], tokens), 1)
    before = jnp.where(cols < rows * CHUNK, 1.0, 0.0).astype(BF16)
    seen = lax.dot_general(
        before, member[...], (((1,), (1,)), ((), ())), preferred_element_type=F32
    )
    seen_ref[...] = seen
    high, low = high_low(sums[:, :DH])
    out_ref[:, :share] = high.reshape(peers, share, DH)
    out_ref[:, share : 2 * share] = low.reshape(peers, share, DH)
    out_ref[:, 2 * share : 3 * share] = sums[:, DH:].astype(BF16).reshape(peers, share, DH)
    counts = seen[tokens // CHUNK : tokens // CHUNK + 1]
    upper = jnp.floor(counts * (1.0 / 16.0)) * 16.0
    lower = counts - upper
    pieces = [
        part[:, k : k + DH] for part in (upper, lower) for k in range(0, CODES, DH)
    ]
    counts_rows = jnp.concatenate(pieces, axis=0).astype(BF16)
    out_ref[:, 3 * share :] = jnp.broadcast_to(
        counts_rows[None], (peers, counts_rows.shape[0], DH)
    )


def combine_kernel(peers, here_ref, parts_ref, out_ref, base_ref):
    share = CODES // peers
    here = here_ref[0]
    counts = parts_ref[:, 3 * share :].astype(F32)
    total = jnp.sum(counts, axis=0)
    place = lax.broadcasted_iota(jnp.int32, counts.shape, 0)
    ahead = jnp.sum(jnp.where(place < here, counts, 0.0), axis=0)
    rows = CODES // DH
    base_ref[...] = ahead[:rows] + ahead[rows:]
    total = total[:rows] + total[rows:]
    code = lax.broadcasted_iota(jnp.int32, (share, DH), 0) + here * share
    lane = lax.broadcasted_iota(jnp.int32, (share, DH), 1)
    mine = jnp.zeros((share, DH), F32)
    for r in range(rows):
        mine = mine + jnp.where(code == lane + r * DH, total[r : r + 1], 0.0)
    mine = jnp.sum(mine, axis=1, keepdims=True)
    key_sums = jnp.sum(parts_ref[:, : 2 * share].astype(F32), axis=0)
    codes = ((key_sums[:share] + key_sums[share:]) / mine).astype(BF16)
    run = jnp.zeros((share, DH), F32)
    for peer in range(peers):
        out_ref[peer, :share] = codes
        out_ref[peer, share:] = run.astype(BF16)
        if peer < peers - 1:
            run = run + parts_ref[peer, 2 * share : 3 * share].astype(F32)


def attend_kernel(
    picks_ref,
    queries_ref,
    values_ref,
    table_ref,
    seen_ref,
    base_ref,
    out_ref,
    squares_ref,
    score_side,
    value_side,
    cache,
    base_row,
    eye,
):
    step = pl.program_id(0)
    share = table_ref.shape[1] // 2
    groups = queries_ref.shape[1] // DH
    lane = lax.broadcasted_iota(jnp.int32, (CODES, DH), 1)
    first_half = lane < DH // 2

    @pl.when(step == 0)
    def _():
        codes = table_ref[:, :share].reshape(CODES, DH)
        score_side[:DH, :CODES] = codes.T
        cache[:, :DH] = table_ref[:, share:].reshape(CODES, DH).astype(F32)
        for r in range(CODES // DH):
            row = base_ref[r : r + 1]
            base_row[:, r * DH : (r + 1) * DH] = row
            cache[r * DH : (r + 1) * DH, DH:] = jnp.broadcast_to(row, (DH, DH)).T
        r = lax.broadcasted_iota(jnp.int32, (CHUNK, CHUNK), 0)
        c = lax.broadcasted_iota(jnp.int32, (CHUNK, CHUNK), 1)
        score_side[DH:, CODES:] = jnp.where(c > r, MASKED, 0.0).astype(BF16)
        eye[...] = jnp.where(c == r, 1.0, 0.0).astype(BF16)
        value_side[CODES:, DH:] = jnp.where(first_half[:CHUNK], 1.0, 0.0).astype(BF16)

    member = one_hot(picks_ref[...], CODES)
    local_keys = jnp.dot(score_side[:DH, :CODES], member, preferred_element_type=F32)
    score_side[:DH, CODES:] = local_keys.astype(BF16)
    present = base_row[...] + seen_ref[pl.ds(step, 1)]
    score_side[DH:, :CODES] = jnp.broadcast_to(
        jnp.where(present > 0.0, 0.0, MASKED), (CHUNK, CODES)
    ).astype(BF16)
    counts = cache[:, DH:]
    upper = jnp.floor(counts * (1.0 / 256.0)) * 256.0
    value_side[:CODES, :DH] = cache[:, :DH].astype(BF16)
    value_side[:CODES, DH:] = jnp.where(first_half, upper, counts - upper).astype(BF16)
    value_side[CODES:, :DH] = values_ref[...]
    ones = jnp.ones((CHUNK, DH), BF16)
    cache[...] += jnp.dot(
        member, jnp.concatenate([values_ref[...], ones], axis=1), preferred_element_type=F32
    )

    squares = jnp.zeros((CHUNK, DH), F32)
    for g in range(groups):
        asked = jnp.concatenate([queries_ref[:, g * DH : (g + 1) * DH], eye[...]], axis=1)
        scores = jnp.dot(asked, score_side[...], preferred_element_type=F32)
        top = jnp.max(scores, axis=1, keepdims=True)
        weights = jnp.exp2((scores - top) * KEEP).astype(BF16)
        mixed = jnp.dot(weights, value_side[...], preferred_element_type=F32)
        tally = mixed[:, DH:]
        attended = mixed[:, :DH] / (tally + pltpu.roll(tally, DH // 2, 1))
        out_ref[:, g * DH : (g + 1) * DH] = attended.astype(out_ref.dtype)
        squares = squares + attended * attended
    pair = jnp.concatenate(high_low(squares), axis=1)
    row = lax.dot_general(
        jnp.ones((8, 2 * DH), BF16), pair, (((1,), (1,)), ((), ())), preferred_element_type=F32
    )[0:1]
    for peer in range(squares_ref.shape[0]):
        squares_ref[peer, pl.ds(step, 1)] = row


def norm_kernel(features, attended_ref, squares_ref, gain_ref, out_ref):
    step = pl.program_id(0)
    chunks = attended_ref.shape[0] // CHUNK
    gain = gain_ref[...]
    for k in range(chunks):
        total = jnp.sum(squares_ref[:, pl.ds(step * chunks + k, 1)], axis=0)
        scale = lax.rsqrt(total * (1.0 / features) + 1e-06)
        scale = jnp.broadcast_to(scale, (DH, CHUNK)).T
        for g in range(attended_ref.shape[1] // DH):
            rows, cols = slice(k * CHUNK, (k + 1) * CHUNK), slice(g * DH, (g + 1) * DH)
            out_ref[rows, cols] = (
                attended_ref[rows, cols].astype(F32) * scale * gain[:, cols]
            ).astype(BF16)


def shape(dims, dtype):
    return jax.ShapeDtypeStruct(dims, dtype)


def local(queries, keys, values, assignments, norm_gain):
    peers = lax.axis_size("seq")
    heads = lax.axis_size("head")
    tokens, width = queries.shape
    chunks = tokens // CHUNK
    share = CODES // peers
    params = functools.partial(pltpu.CompilerParams, vmem_limit_bytes=48 * 2**20)
    count_rows = 2 * CODES // DH

    with jax.named_scope("code_sums"):
        parts, seen = pl.pallas_call(
            functools.partial(sums_kernel, peers),
            out_shape=(
                shape((peers, 3 * share + count_rows, DH), BF16),
                shape((2 * chunks, CODES), F32),
            ),
            scratch_shapes=[pltpu.VMEM((CODES, tokens), BF16), pltpu.VMEM((tokens, 2 * DH), BF16)],
            compiler_params=params(),
        )(assignments, keys, values)
    with jax.named_scope("exchange_sums"):
        parts = lax.all_to_all(parts, "seq", 0, 0)
    with jax.named_scope("combine"):
        here = lax.axis_index("seq").astype(jnp.int32).reshape(1)
        table, base = pl.pallas_call(
            functools.partial(combine_kernel, peers),
            out_shape=(
                shape((peers, 2 * share, DH), BF16),
                shape((CODES // DH, DH), F32),
            ),
            in_specs=[
                pl.BlockSpec(memory_space=pltpu.SMEM),
                pl.BlockSpec(memory_space=pltpu.VMEM),
            ],
            compiler_params=params(),
        )(here, parts)
    with jax.named_scope("exchange_codes"):
        table = lax.all_to_all(table, "seq", 0, 0)
    with jax.named_scope("attend"):
        attended, squares = pl.pallas_call(
            attend_kernel,
            grid=(chunks,),
            in_specs=[
                pl.BlockSpec((1, CHUNK), lambda i: (0, i)),
                pl.BlockSpec((CHUNK, width), lambda i: (i, 0)),
                pl.BlockSpec((CHUNK, DH), lambda i: (i, 0)),
                pl.BlockSpec((peers, 2 * share, DH), lambda i: (0, 0, 0)),
                pl.BlockSpec((2 * chunks, CODES), lambda i: (0, 0)),
                pl.BlockSpec((CODES // DH, DH), lambda i: (0, 0)),
            ],
            out_specs=(
                pl.BlockSpec((CHUNK, width), lambda i: (i, 0)),
                pl.BlockSpec((heads, chunks, CHUNK), lambda i: (0, 0, 0)),
            ),
            out_shape=(
                shape((tokens, width), F32),
                shape((heads, chunks, CHUNK), F32),
            ),
            scratch_shapes=[
                pltpu.VMEM((2 * DH, CODES + CHUNK), BF16),
                pltpu.VMEM((CODES + CHUNK, 2 * DH), BF16),
                pltpu.VMEM((CODES, 2 * DH), F32),
                pltpu.VMEM((1, CODES), F32),
                pltpu.VMEM((CHUNK, CHUNK), BF16),
            ],
            compiler_params=params(dimension_semantics=("arbitrary",)),
        )(assignments, queries, values, table, seen, base)
    with jax.named_scope("exchange_squares"):
        squares = lax.all_to_all(squares, "head", 0, 0)
    with jax.named_scope("norm"):
        step = 4 * CHUNK
        return pl.pallas_call(
            functools.partial(norm_kernel, width * heads),
            grid=(tokens // step,),
            in_specs=[
                pl.BlockSpec((step, width), lambda i: (i, 0)),
                pl.BlockSpec((heads, chunks, CHUNK), lambda i: (0, 0, 0)),
                pl.BlockSpec((1, width), lambda i: (0, 0)),
            ],
            out_specs=pl.BlockSpec((step, width), lambda i: (i, 0)),
            out_shape=shape((tokens, width), BF16),
            compiler_params=params(dimension_semantics=("arbitrary",)),
        )(attended, squares, norm_gain.reshape(1, width))


def solution(mesh):
    in_specs = (P("seq", "head"), P("seq", "head"), P("seq", "head"), P("head", "seq"), P("head"))
    return jax.shard_map(
        local, mesh=mesh, in_specs=in_specs, out_specs=P("seq", "head"), check_vma=False
    )
```

time: 666 us -> 84.9 us (0.13)
  other arithmetic: 195 us -> 0 us
  waiting for transfers between devices: 168 us -> 12.9 us
  blocking collectives: 153 us -> 30 us
  matrix products: 67.9 us -> 0 us
  local copies, waits for them, and re-layouts: 50.3 us -> 5.13 us
  Pallas kernels: 0 us -> 24.6 us
  between operations: 13.4 us -> 0.04 us
    all_gather x2 -> x0, waiting for transfers between devices: 168 us -> none  [carried_in(): everything = jax.tree.map(lambda part: lax.all_gather(part, axis), shard)]
    select_n x66 -> x0, other arithmetic: 110 us -> none  [the longest x64 108 us: turn(): return jax.tree.map(lambda a, b: jnp.where(reached, a, b), new, before)]
    all_gather x2 -> x0, blocking collectives: 77.8 us -> none  [carried_in(): everything = jax.tree.map(lambda part: lax.all_gather(part, axis), shard)]
    dot_general x50 -> x0, matrix products: 67.9 us -> none  [the longest x8 15.7 us: attend_block(): jnp.einsum('hgtj,jhd->thgd', prev_weights.astype(jnp.bfloat16), prev_valu...]
    unnamed x1 -> x0, blocking collectives: 61.8 us -> none
    gt x40 -> x0, other arithmetic: 41.5 us -> none  [the longest x32 41.5 us: combine_totals(): present = later[4] > 0.0]
    reduce_sum x21 -> x0, other arithmetic: 30.6 us -> none  [the longest x8 18 us: attend_block(): jnp.sum(code_weights * cache_counts[:, None, None, :], axis=-1)]
    all_to_all x0 -> x2, blocking collectives: none -> 30 us  [the longest x1 17.3 us: local(): table = lax.all_to_all(table, 'seq', 0, 0)]
  transfers between devices with their start and end apart: 5 -> 1, of which waited for: 2 -> 1; matrix products, arithmetic and copies ran while one was open for 4% -> 0% of each run, Pallas kernels for 0% -> 0%
where the time goes in v1:
time: 84.9 us; the launch traced here: 84.6 us
  blocking collectives  30 us (35%)
  Pallas kernels  24.6 us (29%)
  waiting for transfers between devices  12.9 us (15%)
  starting transfers between devices  11.9 us (14%)
  local copies, waits for them, and re-layouts  5.13 us (6%)
    pallas_call x1, Pallas kernels, local(): pl.pallas_call(attend_kernel, grid=(chunks,), in_specs=[pl.BlockSpec((1,...  20.2 us
    all_to_all x1, blocking collectives, local(): table = lax.all_to_all(table, 'seq', 0, 0)  17.3 us
    all_to_all x1, waiting for transfers between devices, local(): parts = lax.all_to_all(parts, 'seq', 0, 0)  12.9 us
    all_to_all x1, blocking collectives, local(): squares = lax.all_to_all(squares, 'head', 0, 0)  12.7 us
    all_to_all x1, starting transfers between devices, local(): parts = lax.all_to_all(parts, 'seq', 0, 0)  11.9 us
    unnamed x16, local copies, waits for them, and re-layouts  5.13 us
    pallas_call x1, Pallas kernels, local(): pl.pallas_call(functools.partial(norm_kernel, width * heads), grid=(token...  2.22 us
    pallas_call x1, Pallas kernels, local(): pl.pallas_call(functools.partial(sums_kernel, peers), out_shape=(shape((p...  2.1 us
  transfers between devices with their start and end apart: 1, of which 1 were waited for; matrix products, arithmetic and copies ran while one was open for 0% of the time, Pallas kernels for 0%

profile of v1, /device:TPU:1, one launch (start us, length us, event | category | flops | bytes accessed | tf_op | source)
XLA Modules:
  0.0 84.6 jit_solution(3338492045920764638)
XLA Ops:
  0.0 0.0 copy-start.1
  0.0 0.0 copy-start.2
  0.0 1.2 %copy-done.2 = bf16[2048,128]{1,0:T(8,128)(2,1)S(1)} copy-done((bf16[2048,128]{1,0:T(8,128)(2,1)S(1)}, bf16[2048,128]{1,0:T(8,128)(2,1)}, u32[]{:S(2)}) %copy-start.2) | copy-done | bytes 524312
  1.2 0.0 copy-start.4
  1.2 1.0 %copy-done.4 = bf16[2048,128]{1,0:T(8,128)(2,1)S(1)} copy-done((bf16[2048,128]{1,0:T(8,128)(2,1)S(1)}, bf16[2048,128]{1,0:T(8,128)(2,1)}, u32[]{:S(2)}) %copy-start.4) | copy-done | bytes 524312
  2.2 0.0 copy-start.5
  2.2 0.7 copy-done.5
  2.9 0.0 copy-start.3
  2.9 0.0 copy-start.6
  2.9 2.1 %code_sums.1 = (bf16[32,56,128]{2,1,0:T(8,128)(2,1)}, f32[32,512]{1,0:T(8,128)S(1)}) custom-call(s32[1,2048]{1,0:T(1,128)S(1)} %copy-done.5, bf16[2048,128]{1,0:T(8,128)(2,1)S(1)} %copy-done.4, bf16[2048,128]{1,0:T(8,128)(2,1)S(1)} %copy-done.2), custom_call_target="tpu_custom_call" | custom-call | tf_op jit(solution)/shard_map/code_sums/pallas_call | solution.py:188
  5.0 11.9 %all-to-all-start = ((bf16[32,56,128]{2,1,0:T(8,128)(2,1)}), bf16[32,56,128]{2,1,0:T(8,128)(2,1)S(1)}, u32[]{:S(2)}, u32[]{:S(2)}) async-start(bf16[32,56,128]{2,1,0:T(8,128)(2,1)} %get-tuple-element.11), calls=%async_computation | async-start | bytes 917504 | tf_op jit(solution)/shard_map/exchange_sums/all_to_all | solution.py:198
  16.9 0.0 copy-start.7
  16.9 12.9 %all-to-all-done.parts_ref = bf16[32,56,128]{2,1,0:T(8,128)(2,1)S(1)} async-done(((bf16[32,56,128]{2,1,0:T(8,128)(2,1)}), bf16[32,56,128]{2,1,0:T(8,128)(2,1)S(1)}, u32[]{:S(2)}, u32[]{:S(2)}) %all-to-all-start) | async-done | bytes 458784 | tf_op jit(solution)/shard_map/exchange_sums/all_to_all | solution.py:198
  29.8 0.1 combine.1
  30.0 17.3 %all_to_all.15.table_ref = bf16[32,32,128]{2,1,0:T(8,128)(2,1)S(1)} all-to-all(bf16[32,32,128]{2,1,0:T(8,128)(2,1)S(1)} %get-tuple-element.12), channel_id=1, replica_groups=mesh['seq'=32,'head'=8] {'seq'}, dimensions={0} | all-to-all | bytes 524288 | tf_op jit(solution)/shard_map/exchange_codes/all_to_all | solution.py:214
  47.2 0.0 copy-done.1
  47.2 0.0 copy-done.3
  47.2 0.0 copy-done.6
  47.2 20.2 %attend.1 = (f32[2048,512]{1,0:T(8,128)}, f32[8,16,128]{2,1,0:T(8,128)S(1)}) custom-call(s32[1,2048]{1,0:T(1,128)S(1)} %copy-done.6, bf16[2048,512]{1,0:T(8,128)(2,1)S(1)} %copy-done.1, bf16[2048,128]{1,0:T(8,128)(2,1)S(1)} %copy-done.3, bf16[32,32,128]{2,1,0:T(8,128)(2,1)S(1)} %all_to_all.15.table_ref, f32[32,512]{1,0:T(8,128)S(1)} %get-tuple-element.13.seen_ref, ...), custom_call_target="tpu_custom_call" | custom-call | tf_op jit(solution)/shard_map/attend/pallas_call | solution.py:216
  67.4 12.7 %all_to_all.16.squares_ref = f32[8,16,128]{2,1,0:T(8,128)S(1)} all-to-all(f32[8,16,128]{2,1,0:T(8,128)S(1)} %get-tuple-element.16), channel_id=1, replica_groups=mesh['seq'=32,'head'=8] {'head'}, dimensions={0} | all-to-all | bytes 131072 | tf_op jit(solution)/shard_map/exchange_squares/all_to_all | solution.py:245
  80.1 0.0 copy-done.7
  80.1 0.0 copy-start
  80.1 2.2 %copy-done = f32[2048,512]{1,0:T(8,128)S(1)} copy-done((f32[2048,512]{1,0:T(8,128)S(1)}, f32[2048,512]{1,0:T(8,128)}, u32[]{:S(2)}) %copy-start) | copy-done | bytes 4194328
  82.3 2.2 %norm.1 = bf16[2048,512]{1,0:T(8,128)(2,1)} custom-call(f32[2048,512]{1,0:T(8,128)S(1)} %copy-done, f32[8,16,128]{2,1,0:T(8,128)S(1)} %all_to_all.16.squares_ref, f32[1,512]{1,0:T(1,128)S(1)} %bitcast.2), custom_call_target="tpu_custom_call" | custom-call | tf_op jit(solution)/shard_map/norm/pallas_call | solution.py:248
Async XLA Ops:
  0.0 47.2 %copy-start.1 = (bf16[2048,512]{1,0:T(8,128)(2,1)S(1)}, bf16[2048,512]{1,0:T(8,128)(2,1)}, u32[]{:S(2)}) copy-start(bf16[2048,512]{1,0:T(8,128)(2,1)} %queries_ref.1) | copy-start | bytes 6291460
  0.0 1.2 %copy-start.2 = (bf16[2048,128]{1,0:T(8,128)(2,1)S(1)}, bf16[2048,128]{1,0:T(8,128)(2,1)}, u32[]{:S(2)}) copy-start(bf16[2048,128]{1,0:T(8,128)(2,1)} %values_ref.3) | copy-start | bytes 1572868
  1.2 1.0 %copy-start.4 = (bf16[2048,128]{1,0:T(8,128)(2,1)S(1)}, bf16[2048,128]{1,0:T(8,128)(2,1)}, u32[]{:S(2)}) copy-start(bf16[2048,128]{1,0:T(8,128)(2,1)} %keys_ref.1) | copy-start | bytes 1572868
  2.2 0.7 copy-start.5
  2.9 44.3 %copy-start.3 = (bf16[2048,128]{1,0:T(8,128)(2,1)S(1)}, bf16[2048,128]{1,0:T(8,128)(2,1)}, u32[]{:S(2)}) copy-start(bf16[2048,128]{1,0:T(8,128)(2,1)} %values_ref.3) | copy-start | bytes 1572868
  2.9 44.3 %copy-start.6 = (s32[1,2048]{1,0:T(1,128)S(1)}, s32[1,2048]{1,0:T(1,128)}, u32[]{:S(2)}) copy-start(s32[1,2048]{1,0:T(1,128)} %picks_ref.3) | copy-start | bytes 24580
  5.0 24.8 %all-to-all-start = ((bf16[32,56,128]{2,1,0:T(8,128)(2,1)}), bf16[32,56,128]{2,1,0:T(8,128)(2,1)S(1)}, u32[]{:S(2)}, u32[]{:S(2)}) async-start(bf16[32,56,128]{2,1,0:T(8,128)(2,1)} %get-tuple-element.11), calls=%async_computation | async-start | bytes 917504 | tf_op jit(solution)/shard_map/exchange_sums/all_to_all | solution.py:198
  16.9 63.2 %copy-start.7 = (f32[512]{0:T(512)S(1)}, f32[512]{0:T(512)}, u32[]{:S(2)}) copy-start(f32[512]{0:T(512)} %param.9) | copy-start | bytes 6148
  80.1 2.2 %copy-start = (f32[2048,512]{1,0:T(8,128)S(1)}, f32[2048,512]{1,0:T(8,128)}, u32[]{:S(2)}) copy-start(f32[2048,512]{1,0:T(8,128)} %get-tuple-element.15.attended_ref) | copy-start | bytes 12582916

commit v2 on v1

v2 whole, which is shorter than its diff:
```python
import functools
import math

import jax
import jax.numpy as jnp
from jax import lax
from jax.experimental import pallas as pl
from jax.experimental.pallas import tpu as pltpu
from jax.sharding import PartitionSpec as P

DH = 128
CODES = 512
HALF = 128
CHUNK = 2 * HALF
MASKED = -1e30
F32 = jnp.float32
BF16 = jnp.bfloat16
KEEP = 1.0 / math.sqrt(DH) * math.log2(math.e)


def one_hot(picks, rows, first=0):
    ids = lax.broadcasted_iota(jnp.int32, (rows, picks.shape[1]), 0) + first
    return jnp.where(ids == picks, 1.0, 0.0).astype(BF16)


def high_low(x):
    high = x.astype(BF16)
    return high, (x - high.astype(F32)).astype(BF16)


def sums_kernel(
    peers, picks_hbm, keys_hbm, values_hbm, out_ref, seen_ref, member, picks, both, ready
):
    tokens = both.shape[0]
    share = CODES // peers
    copies = (
        pltpu.make_async_copy(picks_hbm, picks, ready.at[0]),
        pltpu.make_async_copy(keys_hbm, both.at[:, :DH], ready.at[1]),
        pltpu.make_async_copy(values_hbm, both.at[:, DH:], ready.at[2]),
    )
    for copy in copies:
        copy.start()
    copies[0].wait()
    for t in range(0, tokens, 512):
        member[:, t : t + 512] = one_hot(picks[:, t : t + 512], CODES)
    copies[1].wait()
    copies[2].wait()
    sums = jnp.dot(member[...], both[...], preferred_element_type=F32)
    rows = lax.broadcasted_iota(jnp.int32, (seen_ref.shape[0], tokens), 0)
    cols = lax.broadcasted_iota(jnp.int32, (seen_ref.shape[0], tokens), 1)
    before = jnp.where(cols < rows * CHUNK, 1.0, 0.0).astype(BF16)
    seen = lax.dot_general(
        before, member[...], (((1,), (1,)), ((), ())), preferred_element_type=F32
    )
    seen_ref[...] = seen
    high, low = high_low(sums[:, :DH])
    out_ref[:, :share] = high.reshape(peers, share, DH)
    out_ref[:, share : 2 * share] = low.reshape(peers, share, DH)
    out_ref[:, 2 * share : 3 * share] = sums[:, DH:].astype(BF16).reshape(peers, share, DH)
    counts = seen[tokens // CHUNK : tokens // CHUNK + 1]
    upper = jnp.floor(counts * (1.0 / 16.0)) * 16.0
    lower = counts - upper
    pieces = [
        part[:, k : k + DH] for part in (upper, lower) for k in range(0, CODES, DH)
    ]
    counts_rows = jnp.concatenate(pieces, axis=0).astype(BF16)
    out_ref[:, 3 * share :] = jnp.broadcast_to(
        counts_rows[None], (peers, counts_rows.shape[0], DH)
    )


def combine_kernel(peers, here_ref, parts_ref, out_ref, base_ref):
    share = CODES // peers
    here = here_ref[0]
    counts = parts_ref[:, 3 * share :].astype(F32)
    total = jnp.sum(counts, axis=0)
    place = lax.broadcasted_iota(jnp.int32, counts.shape, 0)
    ahead = jnp.sum(jnp.where(place < here, counts, 0.0), axis=0)
    rows = CODES // DH
    base_ref[...] = ahead[:rows] + ahead[rows:]
    total = total[:rows] + total[rows:]
    code = lax.broadcasted_iota(jnp.int32, (share, DH), 0) + here * share
    lane = lax.broadcasted_iota(jnp.int32, (share, DH), 1)
    mine = jnp.zeros((share, DH), F32)
    for r in range(rows):
        mine = mine + jnp.where(code == lane + r * DH, total[r : r + 1], 0.0)
    mine = jnp.sum(mine, axis=1, keepdims=True)
    key_sums = jnp.sum(parts_ref[:, : 2 * share].astype(F32), axis=0)
    codes = ((key_sums[:share] + key_sums[share:]) / mine).astype(BF16)
    run = jnp.zeros((share, DH), F32)
    for peer in range(peers):
        out_ref[peer, :share] = codes
        out_ref[peer, share:] = run.astype(BF16)
        if peer < peers - 1:
            run = run + parts_ref[peer, 2 * share : 3 * share].astype(F32)


def prefix_kernel(member_ref, values_ref, out_ref):
    ones = jnp.ones((CHUNK, DH), BF16)
    run = jnp.zeros((CODES, 2 * DH), F32)
    chunks = out_ref.shape[0]
    for i in range(chunks):
        out_ref[i] = run
        if i < chunks - 1:
            rows = slice(i * CHUNK, (i + 1) * CHUNK)
            both = jnp.concatenate([values_ref[rows], ones], axis=1)
            run = run + jnp.dot(member_ref[:, rows], both, preferred_element_type=F32)


def attend_kernel(
    member_ref,
    queries_hbm,
    values_ref,
    table_ref,
    seen_ref,
    base_ref,
    prefix_hbm,
    out_ref,
    squares_ref,
    score_sides,
    value_sides,
    scores,
    weights,
    base,
    squares,
    queries_ref,
    prefix_ref,
    ready,
):
    share = table_ref.shape[1] // 2
    tokens = queries_ref.shape[0]
    groups = queries_ref.shape[1] // DH
    chunks = tokens // CHUNK
    copies = []
    for i in range(chunks):
        rows = slice(i * CHUNK, (i + 1) * CHUNK)
        copies.append(
            (
                pltpu.make_async_copy(queries_hbm.at[rows], queries_ref.at[rows], ready.at[0, i]),
                pltpu.make_async_copy(prefix_hbm.at[i], prefix_ref.at[i], ready.at[1, i]),
            )
        )
        for copy in copies[i]:
            copy.start()
    lane = lax.broadcasted_iota(jnp.int32, (CODES, DH), 1)
    first_half = lane < DH // 2
    r = lax.broadcasted_iota(jnp.int32, (HALF, HALF), 0)
    c = lax.broadcasted_iota(jnp.int32, (HALF, HALF), 1)
    later = jnp.where(c > r, MASKED, 0.0).astype(BF16)
    eye = jnp.where(c == r, 1.0, 0.0).astype(BF16)
    codes_t = table_ref[:, :share].reshape(CODES, DH).T
    base[:, :DH] = table_ref[:, share:].reshape(CODES, DH).astype(F32)
    for k in range(CODES // DH):
        row = base_ref[k : k + 1]
        base[k * DH : (k + 1) * DH, DH:] = jnp.broadcast_to(row, (DH, DH)).T
    base_row = jnp.concatenate([base_ref[k : k + 1] for k in range(CODES // DH)], axis=1)
    for pair in score_sides:
        pair[0][:DH, :CODES] = codes_t
        pair[1][:DH, :CODES] = codes_t
        pair[0][DH:, CODES:] = later
        pair[1][DH:, CODES:] = jnp.concatenate([jnp.zeros_like(later), later], axis=1)
    for side in value_sides:
        side[CODES:, DH:] = jnp.where(first_half[:CHUNK], 1.0, 0.0).astype(BF16)

    def prepare(i):
        early, late = score_sides[i % 2]
        side = value_sides[i % 2]
        rows = slice(i * CHUNK, (i + 1) * CHUNK)
        for copy in copies[i]:
            copy.wait()
        local_keys = jnp.dot(codes_t, member_ref[:, rows], preferred_element_type=F32).astype(BF16)
        early[:DH, CODES:] = local_keys[:, :HALF]
        late[:DH, CODES:] = local_keys
        present = base_row + seen_ref[i : i + 1]
        mask = jnp.broadcast_to(jnp.where(present > 0.0, 0.0, MASKED), (HALF, CODES)).astype(BF16)
        early[DH:, :CODES] = mask
        late[DH:, :CODES] = mask
        cache = base[...] + prefix_ref[i]
        counts = cache[:, DH:]
        upper = jnp.floor(counts * (1.0 / 256.0)) * 256.0
        side[:CODES, :DH] = cache[:, :DH].astype(BF16)
        side[:CODES, DH:] = jnp.where(first_half, upper, counts - upper).astype(BF16)
        side[CODES:, :DH] = values_ref[rows]

    def score(u):
        rows = slice(u * HALF, (u + 1) * HALF)
        asked = jnp.concatenate(
            [
                jnp.concatenate([queries_ref[rows, g * DH : (g + 1) * DH], eye], axis=1)
                for g in range(groups)
            ],
            axis=0,
        )
        side = score_sides[u // 2 % 2][u % 2]
        scores[u % 2][...] = jnp.dot(asked, side[...], preferred_element_type=F32)

    def weigh(u):
        got = scores[u % 2][...]
        top = jnp.max(got, axis=1, keepdims=True)
        weights[u % 2][...] = jnp.exp2((got - top) * KEEP).astype(BF16)

    def mix(u):
        rows = slice(u * HALF, (u + 1) * HALF)
        side = value_sides[u // 2 % 2]
        width = weights[u % 2].shape[1]
        mixed = jnp.dot(weights[u % 2][...], side[:width], preferred_element_type=F32)
        tally = mixed[:, DH:]
        attended = mixed[:, :DH] / (tally + pltpu.roll(tally, DH // 2, 1))
        total = jnp.zeros((HALF, DH), F32)
        for g in range(groups):
            part = attended[g * HALF : (g + 1) * HALF]
            out_ref[rows, g * DH : (g + 1) * DH] = part
            total = total + part * part
        squares[rows, :DH], squares[rows, DH:] = high_low(total)

    units = 2 * chunks
    for t in range(units + 2):
        if 0 <= t - 2:
            mix(t - 2)
        if 0 <= t - 1 < units:
            weigh(t - 1)
        if t < units:
            if t % 2 == 0:
                prepare(t // 2)
            score(t)
    row = lax.dot_general(
        jnp.ones((8, 2 * DH), BF16),
        squares[...],
        (((1,), (1,)), ((), ())),
        preferred_element_type=F32,
    )[0:1]
    lines = jnp.concatenate([row[:, k : k + DH] for k in range(0, tokens, DH)], axis=0)
    squares_ref[...] = jnp.broadcast_to(lines[None], squares_ref.shape)


def norm_kernel(features, attended_ref, squares_ref, gain_ref, out_ref):
    step = pl.program_id(0)
    chunks = attended_ref.shape[0] // HALF
    gain = gain_ref[...]
    for k in range(chunks):
        total = jnp.sum(squares_ref[:, pl.ds(step * chunks + k, 1)], axis=0)
        scale = lax.rsqrt(total * (1.0 / features) + 1e-06)
        scale = jnp.broadcast_to(scale, (DH, HALF)).T
        for g in range(attended_ref.shape[1] // DH):
            rows, cols = slice(k * HALF, (k + 1) * HALF), slice(g * DH, (g + 1) * DH)
            out_ref[rows, cols] = (
                attended_ref[rows, cols].astype(F32) * scale * gain[:, cols]
            ).astype(BF16)


def shape(dims, dtype):
    return jax.ShapeDtypeStruct(dims, dtype)


def in_hbm(x):
    return pltpu.with_memory_space_constraint(x, pltpu.HBM)


def local(queries, keys, values, assignments, norm_gain):
    peers = lax.axis_size("seq")
    heads = lax.axis_size("head")
    tokens, width = queries.shape
    chunks = tokens // CHUNK
    share = CODES // peers
    count_rows = 2 * CODES // DH

    with jax.named_scope("code_sums"):
        parts, seen, member = pl.pallas_call(
            functools.partial(sums_kernel, peers),
            in_specs=[pl.BlockSpec(memory_space=pltpu.HBM)] * 3,
            out_shape=(
                shape((peers, 3 * share + count_rows, DH), BF16),
                shape((2 * chunks, CODES), F32),
                shape((CODES, tokens), BF16),
            ),
            scratch_shapes=[
                pltpu.VMEM((1, tokens), jnp.int32),
                pltpu.VMEM((tokens, 2 * DH), BF16),
                pltpu.SemaphoreType.DMA((3,)),
            ],
            compiler_params=pltpu.CompilerParams(vmem_limit_bytes=12 * 2**20),
        )(in_hbm(assignments), in_hbm(keys), in_hbm(values))
    with jax.named_scope("exchange_sums"):
        parts = lax.all_to_all(parts, "seq", 0, 0)
    with jax.named_scope("combine"):
        here = lax.axis_index("seq").astype(jnp.int32).reshape(1)
        table, base = pl.pallas_call(
            functools.partial(combine_kernel, peers),
            out_shape=(
                shape((peers, 2 * share, DH), BF16),
                shape((CODES // DH, DH), F32),
            ),
            in_specs=[
                pl.BlockSpec(memory_space=pltpu.SMEM),
                pl.BlockSpec(memory_space=pltpu.VMEM),
            ],
            compiler_params=pltpu.CompilerParams(vmem_limit_bytes=8 * 2**20),
        )(here, parts)
    with jax.named_scope("exchange_codes"):
        table = lax.all_to_all(table, "seq", 0, 0)
    with jax.named_scope("prefix"):
        prefix = pl.pallas_call(
            prefix_kernel,
            out_shape=shape((chunks, CODES, 2 * DH), F32),
            compiler_params=pltpu.CompilerParams(vmem_limit_bytes=12 * 2**20),
            cost_estimate=pl.CostEstimate(
                flops=4 * tokens * CODES * DH, bytes_accessed=2**22, transcendentals=0
            ),
        )(member, values)
    with jax.named_scope("attend"):
        groups = width // DH
        attended, squares = pl.pallas_call(
            attend_kernel,
            out_shape=(
                shape((tokens, width), F32),
                shape((heads, tokens // DH, DH), F32),
            ),
            scratch_shapes=[
                [[pltpu.VMEM((2 * DH, CODES + n * HALF), BF16) for n in (1, 2)] for _ in range(2)],
                [pltpu.VMEM((CODES + CHUNK, 2 * DH), BF16) for _ in range(2)],
                [pltpu.VMEM((groups * HALF, CODES + n * HALF), F32) for n in (1, 2)],
                [pltpu.VMEM((groups * HALF, CODES + n * HALF), BF16) for n in (1, 2)],
                pltpu.VMEM((CODES, 2 * DH), F32),
                pltpu.VMEM((tokens, 2 * DH), BF16),
                pltpu.VMEM((tokens, width), BF16),
                pltpu.VMEM((chunks, CODES, 2 * DH), F32),
                pltpu.SemaphoreType.DMA((2, chunks)),
            ],
            in_specs=[
                pl.BlockSpec(memory_space=pltpu.HBM if x in (1, 6) else pltpu.VMEM)
                for x in range(7)
            ],
            compiler_params=pltpu.CompilerParams(vmem_limit_bytes=28 * 2**20),
        )(member, in_hbm(queries), values, table, seen, base, in_hbm(prefix))
    with jax.named_scope("exchange_squares"):
        squares = lax.all_to_all(squares, "head", 0, 0)
    with jax.named_scope("norm"):
        step = 4 * HALF
        return pl.pallas_call(
            functools.partial(norm_kernel, width * heads),
            grid=(tokens // step,),
            in_specs=[
                pl.BlockSpec((step, width), lambda i: (i, 0)),
                pl.BlockSpec((heads, tokens // DH, DH), lambda i: (0, 0, 0)),
                pl.BlockSpec((1, width), lambda i: (0, 0)),
            ],
            out_specs=pl.BlockSpec((step, width), lambda i: (i, 0)),
            out_shape=shape((tokens, width), BF16),
            compiler_params=pltpu.CompilerParams(vmem_limit_bytes=12 * 2**20, dimension_semantics=("arbitrary",)),
        )(attended, squares, norm_gain.reshape(1, width))


def solution(mesh):
    in_specs = (P("seq", "head"), P("seq", "head"), P("seq", "head"), P("head", "seq"), P("head"))
    return jax.shard_map(
        local, mesh=mesh, in_specs=in_specs, out_specs=P("seq", "head"), check_vma=False
    )
```

time: 84.9 us -> 77.8 us (0.916)
  blocking collectives: 30 us -> 12.7 us
  starting transfers between devices: 11.9 us -> 19.8 us
  waiting for transfers between devices: 12.9 us -> 19.8 us
  local copies, waits for them, and re-layouts: 5.13 us -> 1.95 us
  Pallas kernels: 24.6 us -> 23 us
    all_to_all x1 -> x0, blocking collectives: 17.3 us -> none  [local(): table = lax.all_to_all(table, 'seq', 0, 0)]
    all_to_all x0 -> x1, starting transfers between devices: none -> 7.96 us  [local(): table = lax.all_to_all(table, 'seq', 0, 0)]
    all_to_all x0 -> x1, waiting for transfers between devices: none -> 6.88 us  [local(): table = lax.all_to_all(table, 'seq', 0, 0)]
    unnamed x16 -> x6, local copies, waits for them, and re-layouts: 5.13 us -> 1.95 us
    pallas_call x2 -> x3, Pallas kernels: 22.3 us -> 20 us  [the longest x1 16 us: local(): pl.pallas_call(attend_kernel, out_shape=(shape((tokens, width), F32), sha...]
  transfers between devices with their start and end apart: 1 -> 2, of which waited for: 1 -> 2; matrix products, arithmetic and copies ran while one was open for 0% -> 0% of each run, Pallas kernels for 0% -> 1%
where the time goes in v2:
time: 77.8 us; the launch traced here: 77.4 us
  Pallas kernels  23 us (30%)
  starting transfers between devices  19.8 us (25%)
  waiting for transfers between devices  19.8 us (25%)
  blocking collectives  12.7 us (16%)
  local copies, waits for them, and re-layouts  1.95 us (3%)
    pallas_call x1, Pallas kernels, local(): pl.pallas_call(attend_kernel, out_shape=(shape((tokens, width), F32), sha...  16 us
    all_to_all x1, waiting for transfers between devices, local(): parts = lax.all_to_all(parts, 'seq', 0, 0)  12.9 us
    all_to_all x1, blocking collectives, local(): squares = lax.all_to_all(squares, 'head', 0, 0)  12.7 us
    all_to_all x1, starting transfers between devices, local(): parts = lax.all_to_all(parts, 'seq', 0, 0)  11.9 us
    all_to_all x1, starting transfers between devices, local(): table = lax.all_to_all(table, 'seq', 0, 0)  7.96 us
    all_to_all x1, waiting for transfers between devices, local(): table = lax.all_to_all(table, 'seq', 0, 0)  6.88 us
    pallas_call x1, Pallas kernels, local(): pl.pallas_call(functools.partial(sums_kernel, peers), in_specs=[pl.BlockS...  3.3 us
    pallas_call x1, Pallas kernels, local(): pl.pallas_call(functools.partial(norm_kernel, width * heads), grid=(token...  2.22 us
  transfers between devices with their start and end apart: 2, of which 2 were waited for; matrix products, arithmetic and copies ran while one was open for 0% of the time, Pallas kernels for 1%

profile of v2, /device:TPU:1, one launch (start us, length us, event | category | flops | bytes accessed | tf_op | source)
XLA Modules:
  0.0 77.4 jit_solution(9048339800957050549)
XLA Ops:
  0.0 0.0 copy-start.1
  0.0 3.3 %code_sums.1 = (bf16[32,56,128]{2,1,0:T(8,128)(2,1)}, f32[16,512]{1,0:T(8,128)S(1)}, bf16[512,2048]{1,0:T(8,128)(2,1)S(1)}) custom-call(s32[1,2048]{1,0:T(1,128)} %picks_hbm.1, bf16[2048,128]{1,0:T(8,128)(2,1)} %keys_hbm.1, bf16[2048,128]{1,0:T(8,128)(2,1)} %values_ref.3), custom_call_target="tpu_custom_call" | custom-call | tf_op jit(solution)/shard_map/code_sums/pallas_call | solution.py:268
  3.3 11.9 %all-to-all-start = ((bf16[32,56,128]{2,1,0:T(8,128)(2,1)}), bf16[32,56,128]{2,1,0:T(8,128)(2,1)S(1)}, u32[]{:S(2)}, u32[]{:S(2)}) async-start(bf16[32,56,128]{2,1,0:T(8,128)(2,1)} %get-tuple-element.13), calls=%async_computation | async-start | bytes 917504 | tf_op jit(solution)/shard_map/exchange_sums/all_to_all | solution.py:284
  15.2 12.9 %all-to-all-done.parts_ref = bf16[32,56,128]{2,1,0:T(8,128)(2,1)S(1)} async-done(((bf16[32,56,128]{2,1,0:T(8,128)(2,1)}), bf16[32,56,128]{2,1,0:T(8,128)(2,1)S(1)}, u32[]{:S(2)}, u32[]{:S(2)}) %all-to-all-start) | async-done | bytes 458784 | tf_op jit(solution)/shard_map/exchange_sums/all_to_all | solution.py:284
  28.1 0.8 %combine.1 = (bf16[32,32,128]{2,1,0:T(8,128)(2,1)}, f32[4,128]{1,0:T(4,128)S(1)}) custom-call(s32[1]{0:T(128)} %bitcast.here_ref, bf16[32,56,128]{2,1,0:T(8,128)(2,1)S(1)} %all-to-all-done.parts_ref), custom_call_target="tpu_custom_call" | custom-call | tf_op jit(solution)/shard_map/combine/pallas_call | solution.py:287
  28.9 8.0 %all-to-all-start.1 = ((bf16[32,32,128]{2,1,0:T(8,128)(2,1)}), bf16[32,32,128]{2,1,0:T(8,128)(2,1)S(1)}, u32[]{:S(2)}, u32[]{:S(2)}) async-start(bf16[32,32,128]{2,1,0:T(8,128)(2,1)} %get-tuple-element.14), calls=%async_computation.1 | async-start | bytes 524288 | tf_op jit(solution)/shard_map/exchange_codes/all_to_all | solution.py:300
  36.9 0.0 copy-done.1
  36.9 0.6 prefix.1.prefix_hbm
  37.6 0.0 copy-start
  37.6 1.9 %copy-done = f32[8,512,256]{2,1,0:T(8,128)} copy-done((f32[8,512,256]{2,1,0:T(8,128)}, f32[8,512,256]{2,1,0:T(8,128)S(1)}, u32[]{:S(2)}) %copy-start) | copy-done | bytes 4194328
  39.5 6.9 %all-to-all-done.1.table_ref = bf16[32,32,128]{2,1,0:T(8,128)(2,1)S(1)} async-done(((bf16[32,32,128]{2,1,0:T(8,128)(2,1)}), bf16[32,32,128]{2,1,0:T(8,128)(2,1)S(1)}, u32[]{:S(2)}, u32[]{:S(2)}) %all-to-all-start.1) | async-done | bytes 262176 | tf_op jit(solution)/shard_map/exchange_codes/all_to_all | solution.py:300
  46.4 0.0 copy-start.2
  46.4 16.0 %attend.1 = (f32[2048,512]{1,0:T(8,128)S(1)}, f32[8,16,128]{2,1,0:T(8,128)S(1)}) custom-call(bf16[512,2048]{1,0:T(8,128)(2,1)S(1)} %get-tuple-element.12.member_ref, bf16[2048,512]{1,0:T(8,128)(2,1)} %queries_hbm.1, bf16[2048,128]{1,0:T(8,128)(2,1)S(1)} %copy-done.1, bf16[32,32,128]{2,1,0:T(8,128)(2,1)S(1)} %all-to-all-done.1.table_ref, ...), custom_call_target="tpu_custom_call" | custom-call | tf_op jit(solution)/shard_map/attend/pallas_call | solution.py:312
  62.5 12.7 %all_to_all.15.squares_ref = f32[8,16,128]{2,1,0:T(8,128)S(1)} all-to-all(f32[8,16,128]{2,1,0:T(8,128)S(1)} %get-tuple-element.18), channel_id=1, replica_groups=mesh['seq'=32,'head'=8] {'head'}, dimensions={0} | all-to-all | bytes 131072 | tf_op jit(solution)/shard_map/exchange_squares/all_to_all | solution.py:336
  75.2 0.0 copy-done.2
  75.2 2.2 %norm.1 = bf16[2048,512]{1,0:T(8,128)(2,1)} custom-call(f32[2048,512]{1,0:T(8,128)S(1)} %get-tuple-element.17.attended_ref, f32[8,16,128]{2,1,0:T(8,128)S(1)} %all_to_all.15.squares_ref, f32[1,512]{1,0:T(1,128)S(1)} %bitcast.2), custom_call_target="tpu_custom_call" | custom-call | tf_op jit(solution)/shard_map/norm/pallas_call | solution.py:339
Async XLA Ops:
  0.0 36.9 %copy-start.1 = (bf16[2048,128]{1,0:T(8,128)(2,1)S(1)}, bf16[2048,128]{1,0:T(8,128)(2,1)}, u32[]{:S(2)}) copy-start(bf16[2048,128]{1,0:T(8,128)(2,1)} %values_ref.3) | copy-start | bytes 1572868
  3.3 24.8 %all-to-all-start = ((bf16[32,56,128]{2,1,0:T(8,128)(2,1)}), bf16[32,56,128]{2,1,0:T(8,128)(2,1)S(1)}, u32[]{:S(2)}, u32[]{:S(2)}) async-start(bf16[32,56,128]{2,1,0:T(8,128)(2,1)} %get-tuple-element.13), calls=%async_computation | async-start | bytes 917504 | tf_op jit(solution)/shard_map/exchange_sums/all_to_all | solution.py:284
  28.9 17.5 %all-to-all-start.1 = ((bf16[32,32,128]{2,1,0:T(8,128)(2,1)}), bf16[32,32,128]{2,1,0:T(8,128)(2,1)S(1)}, u32[]{:S(2)}, u32[]{:S(2)}) async-start(bf16[32,32,128]{2,1,0:T(8,128)(2,1)} %get-tuple-element.14), calls=%async_computation.1 | async-start | bytes 524288 | tf_op jit(solution)/shard_map/exchange_codes/all_to_all | solution.py:300
  37.6 1.9 %copy-start = (f32[8,512,256]{2,1,0:T(8,128)}, f32[8,512,256]{2,1,0:T(8,128)S(1)}, u32[]{:S(2)}) copy-start(f32[8,512,256]{2,1,0:T(8,128)S(1)} %prefix.1.prefix_hbm) | copy-start | bytes 12582916
  46.4 28.8 %copy-start.2 = (f32[512]{0:T(512)S(1)}, f32[512]{0:T(512)}, u32[]{:S(2)}) copy-start(f32[512]{0:T(512)} %param.9) | copy-start | bytes 6148

commit v3 on v2

v3 whole, which is shorter than its diff:
```python
import functools
import math

import jax
import jax.numpy as jnp
from jax import lax
from jax.experimental import pallas as pl
from jax.experimental.pallas import tpu as pltpu
from jax.sharding import PartitionSpec as P

DH = 128
CODES = 512
CHUNK = 128
PAIR = 2
MASKED = -1e30
F32 = jnp.float32
BF16 = jnp.bfloat16
KEEP = 1.0 / math.sqrt(DH) * math.log2(math.e)


def one_hot(picks, rows, first=0):
    ids = lax.broadcasted_iota(jnp.int32, (rows, picks.shape[1]), 0) + first
    return jnp.where(ids == picks, 1.0, 0.0).astype(BF16)


def high_low(x):
    high = x.astype(BF16)
    return high, (x - high.astype(F32)).astype(BF16)


def sums_kernel(
    peers, picks_hbm, keys_hbm, values_hbm, out_ref, seen_ref, member, picks, both, ready
):
    tokens = both.shape[0]
    share = CODES // peers
    copies = (
        pltpu.make_async_copy(picks_hbm, picks, ready.at[0]),
        pltpu.make_async_copy(keys_hbm, both.at[:, :DH], ready.at[1]),
        pltpu.make_async_copy(values_hbm, both.at[:, DH:], ready.at[2]),
    )
    for copy in copies:
        copy.start()
    copies[0].wait()
    for t in range(0, tokens, 512):
        member[:, t : t + 512] = one_hot(picks[:, t : t + 512], CODES)
    copies[1].wait()
    copies[2].wait()
    sums = jnp.dot(member[...], both[...], preferred_element_type=F32)
    rows = lax.broadcasted_iota(jnp.int32, (seen_ref.shape[0], tokens), 0)
    cols = lax.broadcasted_iota(jnp.int32, (seen_ref.shape[0], tokens), 1)
    before = jnp.where(cols < rows * CHUNK, 1.0, 0.0).astype(BF16)
    seen = lax.dot_general(
        before, member[...], (((1,), (1,)), ((), ())), preferred_element_type=F32
    )
    seen_ref[...] = seen
    high, low = high_low(sums[:, :DH])
    out_ref[:, :share] = high.reshape(peers, share, DH)
    out_ref[:, share : 2 * share] = low.reshape(peers, share, DH)
    out_ref[:, 2 * share : 3 * share] = sums[:, DH:].astype(BF16).reshape(peers, share, DH)
    counts = seen[tokens // CHUNK : tokens // CHUNK + 1]
    upper = jnp.floor(counts * (1.0 / 16.0)) * 16.0
    lower = counts - upper
    pieces = [
        part[:, k : k + DH] for part in (upper, lower) for k in range(0, CODES, DH)
    ]
    counts_rows = jnp.concatenate(pieces, axis=0).astype(BF16)
    out_ref[:, 3 * share :] = jnp.broadcast_to(
        counts_rows[None], (peers, counts_rows.shape[0], DH)
    )


def combine_kernel(peers, here_ref, parts_ref, out_ref, base_ref):
    share = CODES // peers
    here = here_ref[0]
    counts = parts_ref[:, 3 * share :].astype(F32)
    total = jnp.sum(counts, axis=0)
    place = lax.broadcasted_iota(jnp.int32, counts.shape, 0)
    ahead = jnp.sum(jnp.where(place < here, counts, 0.0), axis=0)
    rows = CODES // DH
    base_ref[...] = ahead[:rows] + ahead[rows:]
    total = total[:rows] + total[rows:]
    code = lax.broadcasted_iota(jnp.int32, (share, DH), 0) + here * share
    lane = lax.broadcasted_iota(jnp.int32, (share, DH), 1)
    mine = jnp.zeros((share, DH), F32)
    for r in range(rows):
        mine = mine + jnp.where(code == lane + r * DH, total[r : r + 1], 0.0)
    mine = jnp.sum(mine, axis=1, keepdims=True)
    key_sums = jnp.sum(parts_ref[:, : 2 * share].astype(F32), axis=0)
    codes = ((key_sums[:share] + key_sums[share:]) / mine).astype(BF16)
    run = jnp.zeros((share, DH), F32)
    for peer in range(peers):
        out_ref[peer, :share] = codes
        out_ref[peer, share:] = run.astype(BF16)
        if peer < peers - 1:
            run = run + parts_ref[peer, 2 * share : 3 * share].astype(F32)


def prepare_kernel(member_ref, values_ref, rows_ref, values_t_ref):
    tokens = values_ref.shape[0]
    for k in range(0, tokens, CHUNK):
        rows_ref[k : k + CHUNK] = member_ref[:, k : k + CHUNK].T
        values_t_ref[:, k : k + CHUNK] = values_ref[k : k + CHUNK].T


def attend_kernel(
    queries_hbm,
    rows_hbm,
    values_t_ref,
    table_ref,
    seen_ref,
    base_ref,
    out_ref,
    squares_ref,
    score_sides,
    value_sides,
    scores,
    weights,
    cache,
    counts,
    later,
    queries_ref,
    rows_ref,
    ready,
):
    share = table_ref.shape[1] // 2
    tokens = queries_ref.shape[0]
    groups = queries_ref.shape[1] // DH
    chunks = tokens // CHUNK
    copies = []
    for i in range(chunks):
        rows = slice(i * CHUNK, (i + 1) * CHUNK)
        copies.append(
            (
                pltpu.make_async_copy(queries_hbm.at[rows], queries_ref.at[rows], ready.at[0, i]),
                pltpu.make_async_copy(rows_hbm.at[rows], rows_ref.at[rows], ready.at[1, i]),
            )
        )
        for copy in copies[i]:
            copy.start()
    upper_half = lax.broadcasted_iota(jnp.int32, (16, CODES), 0) < 8
    codes = table_ref[:, :share].reshape(CODES, DH)
    cache[...] = table_ref[:, share:].reshape(CODES, DH).T.astype(F32)
    base_row = jnp.concatenate([base_ref[k : k + 1] for k in range(CODES // DH)], axis=1)
    counts[...] = base_row + seen_ref[:chunks]
    missing = jnp.where(counts[...] > 0.0, 0.0, MASKED)
    missing = jnp.concatenate([missing, jnp.zeros((DH - chunks, CODES), F32)], axis=0)
    for side in score_sides:
        side[:CODES, :DH] = codes
        side[:CODES, DH:] = missing.T.astype(BF16)
        side[CODES:, DH:] = jnp.zeros((CHUNK, DH), BF16)
    for side in value_sides:
        side[DH:, CODES:] = jnp.where(upper_half[:, :CHUNK], 1.0, 0.0).astype(BF16)
    r = lax.broadcasted_iota(jnp.int32, later.shape, 0)
    c = lax.broadcasted_iota(jnp.int32, later.shape, 1)
    later[...] = jnp.where(r > c % CHUNK, MASKED, 0.0)

    def prepare(i):
        score_side, value_side = score_sides[i % 2], value_sides[i % 2]
        rows = slice(i * CHUNK, (i + 1) * CHUNK)
        for copy in copies[i]:
            copy.wait()
        member = rows_ref[rows]
        local_keys = jnp.dot(member, score_side[:CODES, :DH], preferred_element_type=F32)
        score_side[CODES:, :DH] = local_keys.astype(BF16)
        value_side[:DH, :CODES] = cache[...].astype(BF16)
        value_side[:DH, CODES:] = values_t_ref[:, rows]
        upper = jnp.floor(counts[i : i + 1] * (1.0 / 256.0)) * 256.0
        lower = counts[i : i + 1] - upper
        value_side[DH:, :CODES] = jnp.where(upper_half, upper, lower).astype(BF16)
        if i < chunks - 1:
            cache[...] += jnp.dot(values_t_ref[:, rows], member, preferred_element_type=F32)

    per = groups // PAIR
    units = chunks * per

    def place(u):
        i, first = u // per, u % per * PAIR
        return i, slice(i * CHUNK, (i + 1) * CHUNK), range(first, first + PAIR)

    def score(u):
        i, rows, heads = place(u)
        lane = lax.broadcasted_iota(jnp.int32, (CHUNK, DH), 1)
        now = jnp.where(lane == i, 1.0, 0.0).astype(BF16)
        asked = jnp.concatenate(
            [jnp.concatenate([queries_ref[rows, g * DH : (g + 1) * DH], now], axis=1) for g in heads],
            axis=0,
        )
        scores[u % 2][...] = lax.dot_general(
            score_sides[i % 2][...], asked, (((1,), (1,)), ((), ())), preferred_element_type=F32
        )

    def weigh(u):
        far = scores[u % 2][:CODES]
        near = scores[u % 2][CODES:] + later[...]
        top = jnp.maximum(
            jnp.max(far, axis=0, keepdims=True), jnp.max(near, axis=0, keepdims=True)
        )
        weights[u % 2][:CODES] = jnp.exp2((far - top) * KEEP).astype(BF16)
        weights[u % 2][CODES:] = jnp.exp2((near - top) * KEEP).astype(BF16)

    def mix(u):
        i, rows, heads = place(u)
        mixed = jnp.dot(value_sides[i % 2][...], weights[u % 2][...], preferred_element_type=F32)
        tally = mixed[DH : DH + 8] + mixed[DH + 8 :]
        attended = mixed[:DH] * (1.0 / tally)[0:1]
        total = jnp.sum(attended * attended, axis=0, keepdims=True)
        line = total[:, :CHUNK]
        for n, g in enumerate(heads):
            out_ref[rows, g * DH : (g + 1) * DH] = attended[:, n * CHUNK : (n + 1) * CHUNK].T
            if n:
                line = line + total[:, n * CHUNK : (n + 1) * CHUNK]
        if heads[0]:
            line = line + squares_ref[0, i : i + 1]
        if heads[-1] < groups - 1:
            squares_ref[0, i : i + 1] = line
        else:
            for peer in range(squares_ref.shape[0]):
                squares_ref[peer, i : i + 1] = line

    for t in range(units + 2):
        if t < units and t % per == 0:
            prepare(t // per)
        if t < units:
            score(t)
        if 0 <= t - 1 < units:
            weigh(t - 1)
        if 0 <= t - 2:
            mix(t - 2)


def norm_kernel(features, attended_ref, squares_ref, gain_ref, out_hbm, out, ready):
    tokens, width = attended_ref.shape
    total = jnp.sum(squares_ref[...], axis=0)
    scale = lax.rsqrt(total * (1.0 / features) + 1e-06)
    copies = []
    for i in range(tokens // CHUNK):
        rows = slice(i * CHUNK, (i + 1) * CHUNK)
        column = jnp.broadcast_to(scale[i : i + 1], (DH, CHUNK)).T
        for k in range(0, width, DH):
            cols = slice(k, k + DH)
            out[rows, cols] = (attended_ref[rows, cols] * column * gain_ref[:, cols]).astype(BF16)
        copies.append(pltpu.make_async_copy(out.at[rows], out_hbm.at[rows], ready.at[i]))
        copies[i].start()
    for copy in copies:
        copy.wait()


def shape(dims, dtype):
    return jax.ShapeDtypeStruct(dims, dtype)


def in_hbm(x):
    return pltpu.with_memory_space_constraint(x, pltpu.HBM)


def attend(queries, prepared, table, seen, base, heads):
    rows, values_t = prepared
    tokens, width = queries.shape
    chunks = tokens // CHUNK
    keys = CODES + CHUNK
    return pl.pallas_call(
        attend_kernel,
        out_shape=(
            shape((tokens, width), F32),
            shape((heads, chunks, CHUNK), F32),
        ),
        scratch_shapes=[
            [pltpu.VMEM((keys, 2 * DH), BF16) for _ in range(2)],
            [pltpu.VMEM((DH + 16, keys), BF16) for _ in range(2)],
            [pltpu.VMEM((keys, PAIR * CHUNK), F32) for _ in range(2)],
            [pltpu.VMEM((keys, PAIR * CHUNK), BF16) for _ in range(2)],
            pltpu.VMEM((DH, CODES), F32),
            pltpu.VMEM((chunks, CODES), F32),
            pltpu.VMEM((CHUNK, PAIR * CHUNK), F32),
            pltpu.VMEM((tokens, width), BF16),
            pltpu.VMEM((tokens, CODES), BF16),
            pltpu.SemaphoreType.DMA((2, chunks)),
        ],
        in_specs=[
            pl.BlockSpec(memory_space=pltpu.HBM if x < 2 else pltpu.VMEM) for x in range(6)
        ],
        compiler_params=pltpu.CompilerParams(vmem_limit_bytes=20 * 2**20),
    )(in_hbm(queries), in_hbm(rows), values_t, table, seen, base)


def prepare(member, values):
    tokens = values.shape[0]
    return pl.pallas_call(
        prepare_kernel,
        out_shape=(shape((tokens, CODES), BF16), shape((DH, tokens), BF16)),
        compiler_params=pltpu.CompilerParams(vmem_limit_bytes=12 * 2**20),
        cost_estimate=pl.CostEstimate(
            flops=4 * tokens * CODES * DH, bytes_accessed=2**23, transcendentals=0
        ),
    )(member, values)


def local(queries, keys, values, assignments, norm_gain):
    peers = lax.axis_size("seq")
    heads = lax.axis_size("head")
    tokens, width = queries.shape
    chunks = tokens // CHUNK
    share = CODES // peers
    count_rows = 2 * CODES // DH

    with jax.named_scope("code_sums"):
        parts, seen, member = pl.pallas_call(
            functools.partial(sums_kernel, peers),
            in_specs=[pl.BlockSpec(memory_space=pltpu.HBM)] * 3,
            out_shape=(
                shape((peers, 3 * share + count_rows, DH), BF16),
                shape((2 * chunks, CODES), F32),
                shape((CODES, tokens), BF16),
            ),
            scratch_shapes=[
                pltpu.VMEM((1, tokens), jnp.int32),
                pltpu.VMEM((tokens, 2 * DH), BF16),
                pltpu.SemaphoreType.DMA((3,)),
            ],
            compiler_params=pltpu.CompilerParams(vmem_limit_bytes=12 * 2**20),
        )(in_hbm(assignments), in_hbm(keys), in_hbm(values))
    with jax.named_scope("exchange_sums"):
        parts = lax.all_to_all(parts, "seq", 0, 0)
    with jax.named_scope("combine"):
        here = lax.axis_index("seq").astype(jnp.int32).reshape(1)
        table, base = pl.pallas_call(
            functools.partial(combine_kernel, peers),
            out_shape=(
                shape((peers, 2 * share, DH), BF16),
                shape((CODES // DH, DH), F32),
            ),
            in_specs=[
                pl.BlockSpec(memory_space=pltpu.SMEM),
                pl.BlockSpec(memory_space=pltpu.VMEM),
            ],
            compiler_params=pltpu.CompilerParams(vmem_limit_bytes=8 * 2**20),
        )(here, parts)
    with jax.named_scope("exchange_codes"):
        table = lax.all_to_all(table, "seq", 0, 0)
    with jax.named_scope("prepare"):
        prepared = prepare(member, values)
    with jax.named_scope("attend"):
        attended, squares = attend(queries, prepared, table, seen, base, heads)
    with jax.named_scope("exchange_squares"):
        squares = lax.all_to_all(squares, "head", 0, 0)
    with jax.named_scope("norm"):
        return pl.pallas_call(
            functools.partial(norm_kernel, width * heads),
            out_specs=pl.BlockSpec(memory_space=pltpu.HBM),
            out_shape=shape((tokens, width), BF16),
            scratch_shapes=[
                pltpu.VMEM((tokens, width), BF16),
                pltpu.SemaphoreType.DMA((chunks,)),
            ],
            compiler_params=pltpu.CompilerParams(vmem_limit_bytes=12 * 2**20),
        )(attended, squares, norm_gain.reshape(1, width))


def solution(mesh):
    in_specs = (P("seq", "head"), P("seq", "head"), P("seq", "head"), P("head", "seq"), P("head"))
    return jax.shard_map(
        local, mesh=mesh, in_specs=in_specs, out_specs=P("seq", "head"), check_vma=False
    )
```

time: 77.8 us -> 74 us (0.951)
  Pallas kernels: 23 us -> 19.2 us
    pallas_call x3, Pallas kernels: 18.9 us -> 15.1 us  [the longest x1 12.8 us: attend(): pl.pallas_call(attend_kernel, out_shape=(shape((tokens, width), F32), sha...]
where the time goes in v3:
time: 74 us; the launch traced here: 73.7 us
  waiting for transfers between devices  20.3 us (27%)
  starting transfers between devices  19.8 us (27%)
  Pallas kernels  19.2 us (26%)
  blocking collectives  12.7 us (17%)
  local copies, waits for them, and re-layouts  1.32 us (2%)
    all_to_all x1, waiting for transfers between devices, local(): parts = lax.all_to_all(parts, 'seq', 0, 0)  12.9 us
    pallas_call x1, Pallas kernels, attend(): pl.pallas_call(attend_kernel, out_shape=(shape((tokens, width), F32), sha...  12.8 us
    all_to_all x1, blocking collectives, local(): squares = lax.all_to_all(squares, 'head', 0, 0)  12.7 us
    all_to_all x1, starting transfers between devices, local(): parts = lax.all_to_all(parts, 'seq', 0, 0)  11.9 us
    all_to_all x1, starting transfers between devices, local(): table = lax.all_to_all(table, 'seq', 0, 0)  7.96 us
    all_to_all x1, waiting for transfers between devices, local(): table = lax.all_to_all(table, 'seq', 0, 0)  7.42 us
    pallas_call x1, Pallas kernels, local(): pl.pallas_call(functools.partial(sums_kernel, peers), in_specs=[pl.BlockS...  3.3 us
    pallas_call x1, Pallas kernels, local(): pl.pallas_call(functools.partial(norm_kernel, width * heads), out_specs=p...  1.57 us
  transfers between devices with their start and end apart: 2, of which 2 were waited for; matrix products, arithmetic and copies ran while one was open for 0% of the time, Pallas kernels for 1%

profile of v3, /device:TPU:1, one launch (start us, length us, event | category | flops | bytes accessed | tf_op | source)
XLA Modules:
  0.0 73.7 jit_solution(7534379452223309204)
XLA Ops:
  0.0 0.0 copy-start
  0.0 3.3 %code_sums.1 = (bf16[32,56,128]{2,1,0:T(8,128)(2,1)}, f32[32,512]{1,0:T(8,128)S(1)}, bf16[512,2048]{1,0:T(8,128)(2,1)S(1)}) custom-call(s32[1,2048]{1,0:T(1,128)} %picks_hbm.1, bf16[2048,128]{1,0:T(8,128)(2,1)} %keys_hbm.1, bf16[2048,128]{1,0:T(8,128)(2,1)} %values_ref.1), custom_call_target="tpu_custom_call" | custom-call | tf_op jit(solution)/shard_map/code_sums/pallas_call | solution.py:307
  3.3 11.9 %all-to-all-start = ((bf16[32,56,128]{2,1,0:T(8,128)(2,1)}), bf16[32,56,128]{2,1,0:T(8,128)(2,1)S(1)}, u32[]{:S(2)}, u32[]{:S(2)}) async-start(bf16[32,56,128]{2,1,0:T(8,128)(2,1)} %get-tuple-element.17), calls=%async_computation | async-start | bytes 917504 | tf_op jit(solution)/shard_map/exchange_sums/all_to_all | solution.py:323
  15.2 12.9 %all-to-all-done.parts_ref = bf16[32,56,128]{2,1,0:T(8,128)(2,1)S(1)} async-done(((bf16[32,56,128]{2,1,0:T(8,128)(2,1)}), bf16[32,56,128]{2,1,0:T(8,128)(2,1)S(1)}, u32[]{:S(2)}, u32[]{:S(2)}) %all-to-all-start) | async-done | bytes 458784 | tf_op jit(solution)/shard_map/exchange_sums/all_to_all | solution.py:323
  28.1 0.8 %combine.1 = (bf16[32,32,128]{2,1,0:T(8,128)(2,1)}, f32[4,128]{1,0:T(4,128)S(1)}) custom-call(s32[1]{0:T(128)} %bitcast.here_ref, bf16[32,56,128]{2,1,0:T(8,128)(2,1)S(1)} %all-to-all-done.parts_ref), custom_call_target="tpu_custom_call" | custom-call | tf_op jit(solution)/shard_map/combine/pallas_call | solution.py:326
  29.0 8.0 %all-to-all-start.1 = ((bf16[32,32,128]{2,1,0:T(8,128)(2,1)}), bf16[32,32,128]{2,1,0:T(8,128)(2,1)S(1)}, u32[]{:S(2)}, u32[]{:S(2)}) async-start(bf16[32,32,128]{2,1,0:T(8,128)(2,1)} %get-tuple-element.18), calls=%async_computation.1 | async-start | bytes 524288 | tf_op jit(solution)/shard_map/exchange_codes/all_to_all | solution.py:339
  36.9 0.0 copy-done
  36.9 0.7 prepare.1
  37.7 0.0 copy-start.1
  37.7 1.3 %copy-done.1 = bf16[2048,512]{1,0:T(8,128)(2,1)} copy-done((bf16[2048,512]{1,0:T(8,128)(2,1)}, bf16[2048,512]{1,0:T(8,128)(2,1)S(1)}, u32[]{:S(2)}) %copy-start.1) | copy-done | bytes 2097176
  39.0 7.4 %all-to-all-done.1.table_ref = bf16[32,32,128]{2,1,0:T(8,128)(2,1)S(1)} async-done(((bf16[32,32,128]{2,1,0:T(8,128)(2,1)}), bf16[32,32,128]{2,1,0:T(8,128)(2,1)S(1)}, u32[]{:S(2)}, u32[]{:S(2)}) %all-to-all-start.1) | async-done | bytes 262176 | tf_op jit(solution)/shard_map/exchange_codes/all_to_all | solution.py:339
  46.4 0.0 copy-start.2
  46.4 12.8 %attend.1 = (f32[2048,512]{1,0:T(8,128)S(1)}, f32[8,16,128]{2,1,0:T(8,128)S(1)}) custom-call(bf16[2048,512]{1,0:T(8,128)(2,1)} %queries_hbm.1, bf16[2048,512]{1,0:T(8,128)(2,1)} %copy-done.1, bf16[128,2048]{1,0:T(8,128)(2,1)S(1)} %get-tuple-element.16.values_t_ref, bf16[32,32,128]{2,1,0:T(8,128)(2,1)S(1)} %all-to-all-done.1.table_ref, ...), custom_call_target="tpu_custom_call" | custom-call | tf_op jit(solution)/shard_map/attend/pallas_call | solution.py:261
  59.2 12.7 %all_to_all.15.squares_ref = f32[8,16,128]{2,1,0:T(8,128)S(1)} all-to-all(f32[8,16,128]{2,1,0:T(8,128)S(1)} %get-tuple-element.22), channel_id=1, replica_groups=mesh['seq'=32,'head'=8] {'head'}, dimensions={0} | all-to-all | bytes 131072 | tf_op jit(solution)/shard_map/exchange_squares/all_to_all | solution.py:345
  71.9 0.0 copy-done.2
  71.9 1.6 %norm.1 = bf16[2048,512]{1,0:T(8,128)(2,1)} custom-call(f32[2048,512]{1,0:T(8,128)S(1)} %get-tuple-element.21.attended_ref, f32[8,16,128]{2,1,0:T(8,128)S(1)} %all_to_all.15.squares_ref, f32[1,512]{1,0:T(1,128)S(1)} %bitcast.2), custom_call_target="tpu_custom_call" | custom-call | tf_op jit(solution)/shard_map/norm/pallas_call | solution.py:347
Async XLA Ops:
  0.0 36.9 %copy-start = (bf16[2048,128]{1,0:T(8,128)(2,1)S(1)}, bf16[2048,128]{1,0:T(8,128)(2,1)}, u32[]{:S(2)}) copy-start(bf16[2048,128]{1,0:T(8,128)(2,1)} %values_ref.1) | copy-start | bytes 1572868
  3.3 24.8 %all-to-all-start = ((bf16[32,56,128]{2,1,0:T(8,128)(2,1)}), bf16[32,56,128]{2,1,0:T(8,128)(2,1)S(1)}, u32[]{:S(2)}, u32[]{:S(2)}) async-start(bf16[32,56,128]{2,1,0:T(8,128)(2,1)} %get-tuple-element.17), calls=%async_computation | async-start | bytes 917504 | tf_op jit(solution)/shard_map/exchange_sums/all_to_all | solution.py:323
  29.0 17.5 %all-to-all-start.1 = ((bf16[32,32,128]{2,1,0:T(8,128)(2,1)}), bf16[32,32,128]{2,1,0:T(8,128)(2,1)S(1)}, u32[]{:S(2)}, u32[]{:S(2)}) async-start(bf16[32,32,128]{2,1,0:T(8,128)(2,1)} %get-tuple-element.18), calls=%async_computation.1 | async-start | bytes 524288 | tf_op jit(solution)/shard_map/exchange_codes/all_to_all | solution.py:339
  37.7 1.3 %copy-start.1 = (bf16[2048,512]{1,0:T(8,128)(2,1)}, bf16[2048,512]{1,0:T(8,128)(2,1)S(1)}, u32[]{:S(2)}) copy-start(bf16[2048,512]{1,0:T(8,128)(2,1)S(1)} %get-tuple-element.15.rows_hbm) | copy-start | bytes 6291460
  46.4 25.5 %copy-start.2 = (f32[512]{0:T(512)S(1)}, f32[512]{0:T(512)}, u32[]{:S(2)}) copy-start(f32[512]{0:T(512)} %param.9) | copy-start | bytes 6148

commit v4 on v3

--- a/solution.py
+++ b/solution.py
@@ -157,8 +157,6 @@
     def prepare(i):
         score_side, value_side = score_sides[i % 2], value_sides[i % 2]
         rows = slice(i * CHUNK, (i + 1) * CHUNK)
-        for copy in copies[i]:
-            copy.wait()
         member = rows_ref[rows]
         local_keys = jnp.dot(member, score_side[:CODES, :DH], preferred_element_type=F32)
         score_side[CODES:, :DH] = local_keys.astype(BF16)
@@ -217,6 +215,9 @@
             for peer in range(squares_ref.shape[0]):
                 squares_ref[peer, i : i + 1] = line
 
+    for pair in copies:
+        for copy in pair:
+            copy.wait()
     for t in range(units + 2):
         if t < units and t % per == 0:
             prepare(t // per)

time: 74 us -> 73 us (0.986)
  Pallas kernels: 19.2 us -> 18.2 us
    pallas_call x1, Pallas kernels: 12.8 us -> 11.7 us  [attend(): pl.pallas_call(attend_kernel, out_shape=(shape((tokens, width), F32), sha...]
where the time goes in v4:
time: 73 us; the launch traced here: 72.6 us
  waiting for transfers between devices  20.3 us (28%)
  starting transfers between devices  19.8 us (27%)
  Pallas kernels  18.2 us (25%)
  blocking collectives  12.7 us (17%)
  local copies, waits for them, and re-layouts  1.32 us (2%)
    all_to_all x1, waiting for transfers between devices, local(): parts = lax.all_to_all(parts, 'seq', 0, 0)  12.9 us
    all_to_all x1, blocking collectives, local(): squares = lax.all_to_all(squares, 'head', 0, 0)  12.7 us
    all_to_all x1, starting transfers between devices, local(): parts = lax.all_to_all(parts, 'seq', 0, 0)  11.9 us
    pallas_call x1, Pallas kernels, attend(): pl.pallas_call(attend_kernel, out_shape=(shape((tokens, width), F32), sha...  11.7 us
    all_to_all x1, starting transfers between devices, local(): table = lax.all_to_all(table, 'seq', 0, 0)  7.96 us
    all_to_all x1, waiting for transfers between devices, local(): table = lax.all_to_all(table, 'seq', 0, 0)  7.42 us
    pallas_call x1, Pallas kernels, local(): pl.pallas_call(functools.partial(sums_kernel, peers), in_specs=[pl.BlockS...  3.3 us
    pallas_call x1, Pallas kernels, local(): pl.pallas_call(functools.partial(norm_kernel, width * heads), out_specs=p...  1.57 us
  transfers between devices with their start and end apart: 2, of which 2 were waited for; matrix products, arithmetic and copies ran while one was open for 0% of the time, Pallas kernels for 1%

profile of v4, /device:TPU:1, one launch (start us, length us, event | category | flops | bytes accessed | tf_op | source)
XLA Modules:
  0.0 72.6 jit_solution(8054690333289075793)
XLA Ops:
  0.0 0.0 copy-start
  0.0 3.3 %code_sums.1 = (bf16[32,56,128]{2,1,0:T(8,128)(2,1)}, f32[32,512]{1,0:T(8,128)S(1)}, bf16[512,2048]{1,0:T(8,128)(2,1)S(1)}) custom-call(s32[1,2048]{1,0:T(1,128)} %picks_hbm.1, bf16[2048,128]{1,0:T(8,128)(2,1)} %keys_hbm.1, bf16[2048,128]{1,0:T(8,128)(2,1)} %values_ref.1), custom_call_target="tpu_custom_call" | custom-call | tf_op jit(solution)/shard_map/code_sums/pallas_call | solution.py:308
  3.3 11.9 %all-to-all-start = ((bf16[32,56,128]{2,1,0:T(8,128)(2,1)}), bf16[32,56,128]{2,1,0:T(8,128)(2,1)S(1)}, u32[]{:S(2)}, u32[]{:S(2)}) async-start(bf16[32,56,128]{2,1,0:T(8,128)(2,1)} %get-tuple-element.17), calls=%async_computation | async-start | bytes 917504 | tf_op jit(solution)/shard_map/exchange_sums/all_to_all | solution.py:324
  15.2 12.9 %all-to-all-done.parts_ref = bf16[32,56,128]{2,1,0:T(8,128)(2,1)S(1)} async-done(((bf16[32,56,128]{2,1,0:T(8,128)(2,1)}), bf16[32,56,128]{2,1,0:T(8,128)(2,1)S(1)}, u32[]{:S(2)}, u32[]{:S(2)}) %all-to-all-start) | async-done | bytes 458784 | tf_op jit(solution)/shard_map/exchange_sums/all_to_all | solution.py:324
  28.1 0.8 %combine.1 = (bf16[32,32,128]{2,1,0:T(8,128)(2,1)}, f32[4,128]{1,0:T(4,128)S(1)}) custom-call(s32[1]{0:T(128)} %bitcast.here_ref, bf16[32,56,128]{2,1,0:T(8,128)(2,1)S(1)} %all-to-all-done.parts_ref), custom_call_target="tpu_custom_call" | custom-call | tf_op jit(solution)/shard_map/combine/pallas_call | solution.py:327
  29.0 8.0 %all-to-all-start.1 = ((bf16[32,32,128]{2,1,0:T(8,128)(2,1)}), bf16[32,32,128]{2,1,0:T(8,128)(2,1)S(1)}, u32[]{:S(2)}, u32[]{:S(2)}) async-start(bf16[32,32,128]{2,1,0:T(8,128)(2,1)} %get-tuple-element.18), calls=%async_computation.1 | async-start | bytes 524288 | tf_op jit(solution)/shard_map/exchange_codes/all_to_all | solution.py:340
  36.9 0.0 copy-done
  36.9 0.7 %prepare.1 = (bf16[2048,512]{1,0:T(8,128)(2,1)S(1)}, bf16[128,2048]{1,0:T(8,128)(2,1)S(1)}) custom-call(bf16[512,2048]{1,0:T(8,128)(2,1)S(1)} %get-tuple-element.14.member_ref, bf16[2048,128]{1,0:T(8,128)(2,1)S(1)} %copy-done), custom_call_target="tpu_custom_call" | custom-call | flops 536870912 | bytes 8388608 | tf_op jit(solution)/shard_map/prepare/pallas_call | solution.py:289
  37.7 0.0 copy-start.1
  37.7 1.3 %copy-done.1 = bf16[2048,512]{1,0:T(8,128)(2,1)} copy-done((bf16[2048,512]{1,0:T(8,128)(2,1)}, bf16[2048,512]{1,0:T(8,128)(2,1)S(1)}, u32[]{:S(2)}) %copy-start.1) | copy-done | bytes 2097176
  39.0 7.4 %all-to-all-done.1.table_ref = bf16[32,32,128]{2,1,0:T(8,128)(2,1)S(1)} async-done(((bf16[32,32,128]{2,1,0:T(8,128)(2,1)}), bf16[32,32,128]{2,1,0:T(8,128)(2,1)S(1)}, u32[]{:S(2)}, u32[]{:S(2)}) %all-to-all-start.1) | async-done | bytes 262176 | tf_op jit(solution)/shard_map/exchange_codes/all_to_all | solution.py:340
  46.4 0.0 copy-start.2
  46.4 11.7 %attend.1 = (f32[2048,512]{1,0:T(8,128)S(1)}, f32[8,16,128]{2,1,0:T(8,128)S(1)}) custom-call(bf16[2048,512]{1,0:T(8,128)(2,1)} %queries_hbm.1, bf16[2048,512]{1,0:T(8,128)(2,1)} %copy-done.1, bf16[128,2048]{1,0:T(8,128)(2,1)S(1)} %get-tuple-element.16.values_t_ref, bf16[32,32,128]{2,1,0:T(8,128)(2,1)S(1)} %all-to-all-done.1.table_ref, ...), custom_call_target="tpu_custom_call" | custom-call | tf_op jit(solution)/shard_map/attend/pallas_call | solution.py:262
  58.2 12.7 %all_to_all.15.squares_ref = f32[8,16,128]{2,1,0:T(8,128)S(1)} all-to-all(f32[8,16,128]{2,1,0:T(8,128)S(1)} %get-tuple-element.22), channel_id=1, replica_groups=mesh['seq'=32,'head'=8] {'head'}, dimensions={0} | all-to-all | bytes 131072 | tf_op jit(solution)/shard_map/exchange_squares/all_to_all | solution.py:346
  70.9 0.0 copy-done.2
  70.9 1.6 %norm.1 = bf16[2048,512]{1,0:T(8,128)(2,1)} custom-call(f32[2048,512]{1,0:T(8,128)S(1)} %get-tuple-element.21.attended_ref, f32[8,16,128]{2,1,0:T(8,128)S(1)} %all_to_all.15.squares_ref, f32[1,512]{1,0:T(1,128)S(1)} %bitcast.2), custom_call_target="tpu_custom_call" | custom-call | tf_op jit(solution)/shard_map/norm/pallas_call | solution.py:348
Async XLA Ops:
  0.0 36.9 %copy-start = (bf16[2048,128]{1,0:T(8,128)(2,1)S(1)}, bf16[2048,128]{1,0:T(8,128)(2,1)}, u32[]{:S(2)}) copy-start(bf16[2048,128]{1,0:T(8,128)(2,1)} %values_ref.1) | copy-start | bytes 1572868
  3.3 24.8 %all-to-all-start = ((bf16[32,56,128]{2,1,0:T(8,128)(2,1)}), bf16[32,56,128]{2,1,0:T(8,128)(2,1)S(1)}, u32[]{:S(2)}, u32[]{:S(2)}) async-start(bf16[32,56,128]{2,1,0:T(8,128)(2,1)} %get-tuple-element.17), calls=%async_computation | async-start | bytes 917504 | tf_op jit(solution)/shard_map/exchange_sums/all_to_all | solution.py:324
  29.0 17.5 %all-to-all-start.1 = ((bf16[32,32,128]{2,1,0:T(8,128)(2,1)}), bf16[32,32,128]{2,1,0:T(8,128)(2,1)S(1)}, u32[]{:S(2)}, u32[]{:S(2)}) async-start(bf16[32,32,128]{2,1,0:T(8,128)(2,1)} %get-tuple-element.18), calls=%async_computation.1 | async-start | bytes 524288 | tf_op jit(solution)/shard_map/exchange_codes/all_to_all | solution.py:340
  37.7 1.3 %copy-start.1 = (bf16[2048,512]{1,0:T(8,128)(2,1)}, bf16[2048,512]{1,0:T(8,128)(2,1)S(1)}, u32[]{:S(2)}) copy-start(bf16[2048,512]{1,0:T(8,128)(2,1)S(1)} %get-tuple-element.15.rows_hbm) | copy-start | bytes 6291460
  46.4 24.5 %copy-start.2 = (f32[512]{0:T(512)S(1)}, f32[512]{0:T(512)}, u32[]{:S(2)}) copy-start(f32[512]{0:T(512)} %param.9) | copy-start | bytes 6148

commit v5 on v4

--- a/solution.py
+++ b/solution.py
@@ -29,7 +29,7 @@
 
 
 def sums_kernel(
-    peers, picks_hbm, keys_hbm, values_hbm, out_ref, seen_ref, member, picks, both, ready
+    peers, picks_hbm, keys_hbm, values_hbm, out_ref, member, picks, both, ready
 ):
     tokens = both.shape[0]
     share = CODES // peers
@@ -43,21 +43,12 @@
     copies[0].wait()
     for t in range(0, tokens, 512):
         member[:, t : t + 512] = one_hot(picks[:, t : t + 512], CODES)
-    copies[1].wait()
-    copies[2].wait()
-    sums = jnp.dot(member[...], both[...], preferred_element_type=F32)
-    rows = lax.broadcasted_iota(jnp.int32, (seen_ref.shape[0], tokens), 0)
-    cols = lax.broadcasted_iota(jnp.int32, (seen_ref.shape[0], tokens), 1)
-    before = jnp.where(cols < rows * CHUNK, 1.0, 0.0).astype(BF16)
-    seen = lax.dot_general(
-        before, member[...], (((1,), (1,)), ((), ())), preferred_element_type=F32
-    )
-    seen_ref[...] = seen
-    high, low = high_low(sums[:, :DH])
-    out_ref[:, :share] = high.reshape(peers, share, DH)
-    out_ref[:, share : 2 * share] = low.reshape(peers, share, DH)
-    out_ref[:, 2 * share : 3 * share] = sums[:, DH:].astype(BF16).reshape(peers, share, DH)
-    counts = seen[tokens // CHUNK : tokens // CHUNK + 1]
+    counts = lax.dot_general(
+        jnp.ones((16, tokens), BF16),
+        member[...],
+        (((1,), (1,)), ((), ())),
+        preferred_element_type=F32,
+    )[0:1]
     upper = jnp.floor(counts * (1.0 / 16.0)) * 16.0
     lower = counts - upper
     pieces = [
@@ -67,6 +58,13 @@
     out_ref[:, 3 * share :] = jnp.broadcast_to(
         counts_rows[None], (peers, counts_rows.shape[0], DH)
     )
+    copies[1].wait()
+    copies[2].wait()
+    sums = jnp.dot(member[...], both[...], preferred_element_type=F32)
+    high, low = high_low(sums[:, :DH])
+    out_ref[:, :share] = high.reshape(peers, share, DH)
+    out_ref[:, share : 2 * share] = low.reshape(peers, share, DH)
+    out_ref[:, 2 * share : 3 * share] = sums[:, DH:].astype(BF16).reshape(peers, share, DH)
 
 
 def combine_kernel(peers, here_ref, parts_ref, out_ref, base_ref):
@@ -95,11 +93,25 @@
             run = run + parts_ref[peer, 2 * share : 3 * share].astype(F32)
 
 
-def prepare_kernel(member_ref, values_ref, rows_ref, values_t_ref):
+def prepare_kernel(
+    member_ref, values_ref, base_ref, rows_ref, values_t_ref, missing_ref, counts_ref
+):
     tokens = values_ref.shape[0]
+    chunks = tokens // CHUNK
     for k in range(0, tokens, CHUNK):
         rows_ref[k : k + CHUNK] = member_ref[:, k : k + CHUNK].T
         values_t_ref[:, k : k + CHUNK] = values_ref[k : k + CHUNK].T
+    base_row = jnp.concatenate([base_ref[k : k + 1] for k in range(CODES // DH)], axis=1)
+    rows = lax.broadcasted_iota(jnp.int32, (chunks, tokens), 0)
+    cols = lax.broadcasted_iota(jnp.int32, (chunks, tokens), 1)
+    before = jnp.where(cols < rows * CHUNK, 1.0, 0.0).astype(BF16)
+    counts = base_row + lax.dot_general(
+        before, member_ref[...], (((1,), (1,)), ((), ())), preferred_element_type=F32
+    )
+    counts_ref[...] = counts
+    missing = jnp.where(counts > 0.0, 0.0, MASKED)
+    missing = jnp.concatenate([missing, jnp.zeros((DH - chunks, CODES), F32)], axis=0)
+    missing_ref[...] = missing.T.astype(BF16)
 
 
 def attend_kernel(
@@ -107,8 +119,8 @@
     rows_hbm,
     values_t_ref,
     table_ref,
-    seen_ref,
-    base_ref,
+    missing_ref,
+    counts_hbm,
     out_ref,
     squares_ref,
     score_sides,
@@ -116,16 +128,18 @@
     scores,
     weights,
     cache,
-    counts,
     later,
     queries_ref,
     rows_ref,
+    counts_ref,
     ready,
 ):
     share = table_ref.shape[1] // 2
     tokens = queries_ref.shape[0]
     groups = queries_ref.shape[1] // DH
     chunks = tokens // CHUNK
+    tally_copy = pltpu.make_async_copy(counts_hbm, counts_ref, ready.at[0, chunks])
+    tally_copy.start()
     copies = []
     for i in range(chunks):
         rows = slice(i * CHUNK, (i + 1) * CHUNK)
@@ -140,13 +154,9 @@
     upper_half = lax.broadcasted_iota(jnp.int32, (16, CODES), 0) < 8
     codes = table_ref[:, :share].reshape(CODES, DH)
     cache[...] = table_ref[:, share:].reshape(CODES, DH).T.astype(F32)
-    base_row = jnp.concatenate([base_ref[k : k + 1] for k in range(CODES // DH)], axis=1)
-    counts[...] = base_row + seen_ref[:chunks]
-    missing = jnp.where(counts[...] > 0.0, 0.0, MASKED)
-    missing = jnp.concatenate([missing, jnp.zeros((DH - chunks, CODES), F32)], axis=0)
     for side in score_sides:
         side[:CODES, :DH] = codes
-        side[:CODES, DH:] = missing.T.astype(BF16)
+        side[:CODES, DH:] = missing_ref[...]
         side[CODES:, DH:] = jnp.zeros((CHUNK, DH), BF16)
     for side in value_sides:
         side[DH:, CODES:] = jnp.where(upper_half[:, :CHUNK], 1.0, 0.0).astype(BF16)
@@ -162,8 +172,8 @@
         score_side[CODES:, :DH] = local_keys.astype(BF16)
         value_side[:DH, :CODES] = cache[...].astype(BF16)
         value_side[:DH, CODES:] = values_t_ref[:, rows]
-        upper = jnp.floor(counts[i : i + 1] * (1.0 / 256.0)) * 256.0
-        lower = counts[i : i + 1] - upper
+        upper = jnp.floor(counts_ref[i : i + 1] * (1.0 / 256.0)) * 256.0
+        lower = counts_ref[i : i + 1] - upper
         value_side[DH:, :CODES] = jnp.where(upper_half, upper, lower).astype(BF16)
         if i < chunks - 1:
             cache[...] += jnp.dot(values_t_ref[:, rows], member, preferred_element_type=F32)
@@ -215,6 +225,7 @@
             for peer in range(squares_ref.shape[0]):
                 squares_ref[peer, i : i + 1] = line
 
+    tally_copy.wait()
     for pair in copies:
         for copy in pair:
             copy.wait()
@@ -254,8 +265,8 @@
     return pltpu.with_memory_space_constraint(x, pltpu.HBM)
 
 
-def attend(queries, prepared, table, seen, base, heads):
-    rows, values_t = prepared
+def attend(queries, prepared, table, heads):
+    rows, values_t, missing, counts = prepared
     tokens, width = queries.shape
     chunks = tokens // CHUNK
     keys = CODES + CHUNK
@@ -271,29 +282,35 @@
             [pltpu.VMEM((keys, PAIR * CHUNK), F32) for _ in range(2)],
             [pltpu.VMEM((keys, PAIR * CHUNK), BF16) for _ in range(2)],
             pltpu.VMEM((DH, CODES), F32),
-            pltpu.VMEM((chunks, CODES), F32),
             pltpu.VMEM((CHUNK, PAIR * CHUNK), F32),
             pltpu.VMEM((tokens, width), BF16),
             pltpu.VMEM((tokens, CODES), BF16),
-            pltpu.SemaphoreType.DMA((2, chunks)),
+            pltpu.VMEM((chunks, CODES), F32),
+            pltpu.SemaphoreType.DMA((2, chunks + 1)),
         ],
         in_specs=[
-            pl.BlockSpec(memory_space=pltpu.HBM if x < 2 else pltpu.VMEM) for x in range(6)
+            pl.BlockSpec(memory_space=pltpu.HBM if x in (0, 1, 5) else pltpu.VMEM) for x in range(6)
         ],
         compiler_params=pltpu.CompilerParams(vmem_limit_bytes=20 * 2**20),
-    )(in_hbm(queries), in_hbm(rows), values_t, table, seen, base)
-
-
-def prepare(member, values):
+    )(in_hbm(queries), in_hbm(rows), values_t, table, missing, in_hbm(counts))
+
+
+def prepare(member, values, base):
     tokens = values.shape[0]
+    chunks = tokens // CHUNK
     return pl.pallas_call(
         prepare_kernel,
-        out_shape=(shape((tokens, CODES), BF16), shape((DH, tokens), BF16)),
+        out_shape=(
+            shape((tokens, CODES), BF16),
+            shape((DH, tokens), BF16),
+            shape((CODES, DH), BF16),
+            shape((chunks, CODES), F32),
+        ),
         compiler_params=pltpu.CompilerParams(vmem_limit_bytes=12 * 2**20),
         cost_estimate=pl.CostEstimate(
             flops=4 * tokens * CODES * DH, bytes_accessed=2**23, transcendentals=0
         ),
-    )(member, values)
+    )(member, values, base)
 
 
 def local(queries, keys, values, assignments, norm_gain):
@@ -305,12 +322,11 @@
     count_rows = 2 * CODES // DH
 
     with jax.named_scope("code_sums"):
-        parts, seen, member = pl.pallas_call(
+        parts, member = pl.pallas_call(
             functools.partial(sums_kernel, peers),
             in_specs=[pl.BlockSpec(memory_space=pltpu.HBM)] * 3,
             out_shape=(
                 shape((peers, 3 * share + count_rows, DH), BF16),
-                shape((2 * chunks, CODES), F32),
                 shape((CODES, tokens), BF16),
             ),
             scratch_shapes=[
@@ -339,9 +355,9 @@
     with jax.named_scope("exchange_codes"):
         table = lax.all_to_all(table, "seq", 0, 0)
     with jax.named_scope("prepare"):
-        prepared = prepare(member, values)
+        prepared = prepare(member, values, base)
     with jax.named_scope("attend"):
-        attended, squares = attend(queries, prepared, table, seen, base, heads)
+        attended, squares = attend(queries, prepared, table, heads)
     with jax.named_scope("exchange_squares"):
         squares = lax.all_to_all(squares, "head", 0, 0)
     with jax.named_scope("norm"):

time: 73 us -> 73 us (level)
    unnamed x6 -> x8, local copies, waits for them, and re-layouts: 1.32 us -> 1.92 us
where the time goes in v5:
time: 73 us; the launch traced here: 72.6 us
  starting transfers between devices  19.8 us (27%)
  waiting for transfers between devices  19.7 us (27%)
  Pallas kernels  18.3 us (25%)
  blocking collectives  12.7 us (17%)
  local copies, waits for them, and re-layouts  1.92 us (3%)
    all_to_all x1, waiting for transfers between devices, local(): parts = lax.all_to_all(parts, 'seq', 0, 0)  12.9 us
    all_to_all x1, blocking collectives, local(): squares = lax.all_to_all(squares, 'head', 0, 0)  12.7 us
    all_to_all x1, starting transfers between devices, local(): parts = lax.all_to_all(parts, 'seq', 0, 0)  11.9 us
    pallas_call x1, Pallas kernels, attend(): pl.pallas_call(attend_kernel, out_shape=(shape((tokens, width), F32), sha...  11.8 us
    all_to_all x1, starting transfers between devices, local(): table = lax.all_to_all(table, 'seq', 0, 0)  7.96 us
    all_to_all x1, waiting for transfers between devices, local(): table = lax.all_to_all(table, 'seq', 0, 0)  6.75 us
    pallas_call x1, Pallas kernels, local(): pl.pallas_call(functools.partial(sums_kernel, peers), in_specs=[pl.BlockS...  3.24 us
    unnamed x8, local copies, waits for them, and re-layouts  1.92 us
  transfers between devices with their start and end apart: 2, of which 2 were waited for; matrix products, arithmetic and copies ran while one was open for 0% of the time, Pallas kernels for 1%

profile of v5, /device:TPU:1, one launch (start us, length us, event | category | flops | bytes accessed | tf_op | source)
XLA Modules:
  0.0 72.6 jit_solution(13834591700645586440)
XLA Ops:
  0.0 0.0 copy-start.1
  0.0 3.2 %code_sums.1 = (bf16[32,56,128]{2,1,0:T(8,128)(2,1)}, bf16[512,2048]{1,0:T(8,128)(2,1)S(1)}) custom-call(s32[1,2048]{1,0:T(1,128)} %picks_hbm.1, bf16[2048,128]{1,0:T(8,128)(2,1)} %keys_hbm.1, bf16[2048,128]{1,0:T(8,128)(2,1)} %values_ref.1), custom_call_target="tpu_custom_call" | custom-call | tf_op jit(solution)/shard_map/code_sums/pallas_call | solution.py:325
  3.3 11.9 %all-to-all-start = ((bf16[32,56,128]{2,1,0:T(8,128)(2,1)}), bf16[32,56,128]{2,1,0:T(8,128)(2,1)S(1)}, u32[]{:S(2)}, u32[]{:S(2)}) async-start(bf16[32,56,128]{2,1,0:T(8,128)(2,1)} %get-tuple-element.16), calls=%async_computation | async-start | bytes 917504 | tf_op jit(solution)/shard_map/exchange_sums/all_to_all | solution.py:340
  15.1 12.9 %all-to-all-done.parts_ref = bf16[32,56,128]{2,1,0:T(8,128)(2,1)S(1)} async-done(((bf16[32,56,128]{2,1,0:T(8,128)(2,1)}), bf16[32,56,128]{2,1,0:T(8,128)(2,1)S(1)}, u32[]{:S(2)}, u32[]{:S(2)}) %all-to-all-start) | async-done | bytes 458784 | tf_op jit(solution)/shard_map/exchange_sums/all_to_all | solution.py:340
  28.0 0.8 %combine.1 = (bf16[32,32,128]{2,1,0:T(8,128)(2,1)}, f32[4,128]{1,0:T(4,128)S(1)}) custom-call(s32[1]{0:T(128)} %bitcast.here_ref, bf16[32,56,128]{2,1,0:T(8,128)(2,1)S(1)} %all-to-all-done.parts_ref), custom_call_target="tpu_custom_call" | custom-call | tf_op jit(solution)/shard_map/combine/pallas_call | solution.py:343
  28.9 8.0 %all-to-all-start.1 = ((bf16[32,32,128]{2,1,0:T(8,128)(2,1)}), bf16[32,32,128]{2,1,0:T(8,128)(2,1)S(1)}, u32[]{:S(2)}, u32[]{:S(2)}) async-start(bf16[32,32,128]{2,1,0:T(8,128)(2,1)} %get-tuple-element.20), calls=%async_computation.1 | async-start | bytes 524288 | tf_op jit(solution)/shard_map/exchange_codes/all_to_all | solution.py:356
  36.9 0.0 copy-done.1
  36.9 0.8 %prepare.1 = (bf16[2048,512]{1,0:T(8,128)(2,1)S(1)}, bf16[128,2048]{1,0:T(8,128)(2,1)S(1)}, bf16[512,128]{1,0:T(8,128)(2,1)S(1)}, f32[16,512]{1,0:T(8,128)S(1)}) custom-call(bf16[512,2048]{1,0:T(8,128)(2,1)S(1)} %get-tuple-element.15.member_ref, bf16[2048,128]{1,0:T(8,128)(2,1)S(1)} %copy-done.1, f32[4,128]{1,0:T(4,128)S(1)} %get-tuple-element.17.base_ref), custom_call_target="tpu_custom_call" | custom-call | flops 536870912 | bytes 8388608 | tf_op jit(solution)/shard_map/prepare/pallas_call | solution.py:301
  37.7 0.0 copy-start
  37.7 1.3 %copy-done = bf16[2048,512]{1,0:T(8,128)(2,1)} copy-done((bf16[2048,512]{1,0:T(8,128)(2,1)}, bf16[2048,512]{1,0:T(8,128)(2,1)S(1)}, u32[]{:S(2)}) %copy-start) | copy-done | bytes 2097176
  39.0 0.0 copy-start.2
  39.0 0.6 copy-done.2
  39.6 6.7 %all-to-all-done.1.table_ref = bf16[32,32,128]{2,1,0:T(8,128)(2,1)S(1)} async-done(((bf16[32,32,128]{2,1,0:T(8,128)(2,1)}), bf16[32,32,128]{2,1,0:T(8,128)(2,1)S(1)}, u32[]{:S(2)}, u32[]{:S(2)}) %all-to-all-start.1) | async-done | bytes 262176 | tf_op jit(solution)/shard_map/exchange_codes/all_to_all | solution.py:356
  46.4 0.0 copy-start.3
  46.4 11.8 %attend.1 = (f32[2048,512]{1,0:T(8,128)S(1)}, f32[8,16,128]{2,1,0:T(8,128)S(1)}) custom-call(bf16[2048,512]{1,0:T(8,128)(2,1)} %queries_hbm.1, bf16[2048,512]{1,0:T(8,128)(2,1)} %copy-done, bf16[128,2048]{1,0:T(8,128)(2,1)S(1)} %get-tuple-element.19.values_t_ref, bf16[32,32,128]{2,1,0:T(8,128)(2,1)S(1)} %all-to-all-done.1.table_ref, ...), custom_call_target="tpu_custom_call" | custom-call | tf_op jit(solution)/shard_map/attend/pallas_call | solution.py:273
  58.2 12.7 %all_to_all.15.squares_ref = f32[8,16,128]{2,1,0:T(8,128)S(1)} all-to-all(f32[8,16,128]{2,1,0:T(8,128)S(1)} %get-tuple-element.24), channel_id=1, replica_groups=mesh['seq'=32,'head'=8] {'head'}, dimensions={0} | all-to-all | bytes 131072 | tf_op jit(solution)/shard_map/exchange_squares/all_to_all | solution.py:362
  70.9 0.0 copy-done.3
  70.9 1.6 %norm.1 = bf16[2048,512]{1,0:T(8,128)(2,1)} custom-call(f32[2048,512]{1,0:T(8,128)S(1)} %get-tuple-element.23.attended_ref, f32[8,16,128]{2,1,0:T(8,128)S(1)} %all_to_all.15.squares_ref, f32[1,512]{1,0:T(1,128)S(1)} %bitcast.2), custom_call_target="tpu_custom_call" | custom-call | tf_op jit(solution)/shard_map/norm/pallas_call | solution.py:364
Async XLA Ops:
  0.0 36.9 %copy-start.1 = (bf16[2048,128]{1,0:T(8,128)(2,1)S(1)}, bf16[2048,128]{1,0:T(8,128)(2,1)}, u32[]{:S(2)}) copy-start(bf16[2048,128]{1,0:T(8,128)(2,1)} %values_ref.1) | copy-start | bytes 1572868
  3.3 24.8 %all-to-all-start = ((bf16[32,56,128]{2,1,0:T(8,128)(2,1)}), bf16[32,56,128]{2,1,0:T(8,128)(2,1)S(1)}, u32[]{:S(2)}, u32[]{:S(2)}) async-start(bf16[32,56,128]{2,1,0:T(8,128)(2,1)} %get-tuple-element.16), calls=%async_computation | async-start | bytes 917504 | tf_op jit(solution)/shard_map/exchange_sums/all_to_all | solution.py:340
  28.9 17.5 %all-to-all-start.1 = ((bf16[32,32,128]{2,1,0:T(8,128)(2,1)}), bf16[32,32,128]{2,1,0:T(8,128)(2,1)S(1)}, u32[]{:S(2)}, u32[]{:S(2)}) async-start(bf16[32,32,128]{2,1,0:T(8,128)(2,1)} %get-tuple-element.20), calls=%async_computation.1 | async-start | bytes 524288 | tf_op jit(solution)/shard_map/exchange_codes/all_to_all | solution.py:356
  37.7 1.3 %copy-start = (bf16[2048,512]{1,0:T(8,128)(2,1)}, bf16[2048,512]{1,0:T(8,128)(2,1)S(1)}, u32[]{:S(2)}) copy-start(bf16[2048,512]{1,0:T(8,128)(2,1)S(1)} %get-tuple-element.18.rows_hbm) | copy-start | bytes 6291460
  39.0 0.6 copy-start.2
  46.4 24.5 %copy-start.3 = (f32[512]{0:T(512)S(1)}, f32[512]{0:T(512)}, u32[]{:S(2)}) copy-start(f32[512]{0:T(512)} %param.9) | copy-start | bytes 6148

commit v6 on v5

--- a/solution.py
+++ b/solution.py
@@ -226,10 +226,11 @@
                 squares_ref[peer, i : i + 1] = line
 
     tally_copy.wait()
-    for pair in copies:
-        for copy in pair:
-            copy.wait()
     for t in range(units + 2):
+        if t in (0, 2 * per):
+            for pair in copies[:2] if t == 0 else copies[2:]:
+                for copy in pair:
+                    copy.wait()
         if t < units and t % per == 0:
             prepare(t // per)
         if t < units:

time: 73 us -> 71.6 us (0.981)
  Pallas kernels: 18.3 us -> 16.9 us
    pallas_call x1, Pallas kernels: 11.8 us -> 10.5 us  [attend(): pl.pallas_call(attend_kernel, out_shape=(shape((tokens, width), F32), sha...]
where the time goes in v6:
time: 71.6 us; the launch traced here: 71.3 us
  starting transfers between devices  19.8 us (28%)
  waiting for transfers between devices  19.7 us (28%)
  Pallas kernels  16.9 us (24%)
  blocking collectives  12.7 us (18%)
  local copies, waits for them, and re-layouts  1.92 us (3%)
    all_to_all x1, waiting for transfers between devices, local(): parts = lax.all_to_all(parts, 'seq', 0, 0)  12.9 us
    all_to_all x1, blocking collectives, local(): squares = lax.all_to_all(squares, 'head', 0, 0)  12.7 us
    all_to_all x1, starting transfers between devices, local(): parts = lax.all_to_all(parts, 'seq', 0, 0)  11.9 us
    pallas_call x1, Pallas kernels, attend(): pl.pallas_call(attend_kernel, out_shape=(shape((tokens, width), F32), sha...  10.5 us
    all_to_all x1, starting transfers between devices, local(): table = lax.all_to_all(table, 'seq', 0, 0)  7.96 us
    all_to_all x1, waiting for transfers between devices, local(): table = lax.all_to_all(table, 'seq', 0, 0)  6.75 us
    pallas_call x1, Pallas kernels, local(): pl.pallas_call(functools.partial(sums_kernel, peers), in_specs=[pl.BlockS...  3.24 us
    unnamed x8, local copies, waits for them, and re-layouts  1.92 us
  transfers between devices with their start and end apart: 2, of which 2 were waited for; matrix products, arithmetic and copies ran while one was open for 0% of the time, Pallas kernels for 1%

profile of v6, /device:TPU:1, one launch (start us, length us, event | category | flops | bytes accessed | tf_op | source)
XLA Modules:
  0.0 71.3 jit_solution(11114871199707319523)
XLA Ops:
  0.0 0.0 copy-start.1
  0.0 3.2 %code_sums.1 = (bf16[32,56,128]{2,1,0:T(8,128)(2,1)}, bf16[512,2048]{1,0:T(8,128)(2,1)S(1)}) custom-call(s32[1,2048]{1,0:T(1,128)} %picks_hbm.1, bf16[2048,128]{1,0:T(8,128)(2,1)} %keys_hbm.1, bf16[2048,128]{1,0:T(8,128)(2,1)} %values_ref.1), custom_call_target="tpu_custom_call" | custom-call | tf_op jit(solution)/shard_map/code_sums/pallas_call | solution.py:326
  3.3 11.9 %all-to-all-start = ((bf16[32,56,128]{2,1,0:T(8,128)(2,1)}), bf16[32,56,128]{2,1,0:T(8,128)(2,1)S(1)}, u32[]{:S(2)}, u32[]{:S(2)}) async-start(bf16[32,56,128]{2,1,0:T(8,128)(2,1)} %get-tuple-element.16), calls=%async_computation | async-start | bytes 917504 | tf_op jit(solution)/shard_map/exchange_sums/all_to_all | solution.py:341
  15.1 12.9 %all-to-all-done.parts_ref = bf16[32,56,128]{2,1,0:T(8,128)(2,1)S(1)} async-done(((bf16[32,56,128]{2,1,0:T(8,128)(2,1)}), bf16[32,56,128]{2,1,0:T(8,128)(2,1)S(1)}, u32[]{:S(2)}, u32[]{:S(2)}) %all-to-all-start) | async-done | bytes 458784 | tf_op jit(solution)/shard_map/exchange_sums/all_to_all | solution.py:341
  28.0 0.8 %combine.1 = (bf16[32,32,128]{2,1,0:T(8,128)(2,1)}, f32[4,128]{1,0:T(4,128)S(1)}) custom-call(s32[1]{0:T(128)} %bitcast.here_ref, bf16[32,56,128]{2,1,0:T(8,128)(2,1)S(1)} %all-to-all-done.parts_ref), custom_call_target="tpu_custom_call" | custom-call | tf_op jit(solution)/shard_map/combine/pallas_call | solution.py:344
  28.9 8.0 %all-to-all-start.1 = ((bf16[32,32,128]{2,1,0:T(8,128)(2,1)}), bf16[32,32,128]{2,1,0:T(8,128)(2,1)S(1)}, u32[]{:S(2)}, u32[]{:S(2)}) async-start(bf16[32,32,128]{2,1,0:T(8,128)(2,1)} %get-tuple-element.20), calls=%async_computation.1 | async-start | bytes 524288 | tf_op jit(solution)/shard_map/exchange_codes/all_to_all | solution.py:357
  36.9 0.0 copy-done.1
  36.9 0.8 %prepare.1 = (bf16[2048,512]{1,0:T(8,128)(2,1)S(1)}, bf16[128,2048]{1,0:T(8,128)(2,1)S(1)}, bf16[512,128]{1,0:T(8,128)(2,1)S(1)}, f32[16,512]{1,0:T(8,128)S(1)}) custom-call(bf16[512,2048]{1,0:T(8,128)(2,1)S(1)} %get-tuple-element.15.member_ref, bf16[2048,128]{1,0:T(8,128)(2,1)S(1)} %copy-done.1, f32[4,128]{1,0:T(4,128)S(1)} %get-tuple-element.17.base_ref), custom_call_target="tpu_custom_call" | custom-call | flops 536870912 | bytes 8388608 | tf_op jit(solution)/shard_map/prepare/pallas_call | solution.py:302
  37.7 0.0 copy-start
  37.7 1.3 %copy-done = bf16[2048,512]{1,0:T(8,128)(2,1)} copy-done((bf16[2048,512]{1,0:T(8,128)(2,1)}, bf16[2048,512]{1,0:T(8,128)(2,1)S(1)}, u32[]{:S(2)}) %copy-start) | copy-done | bytes 2097176
  39.0 0.0 copy-start.2
  39.0 0.6 copy-done.2
  39.6 6.7 %all-to-all-done.1.table_ref = bf16[32,32,128]{2,1,0:T(8,128)(2,1)S(1)} async-done(((bf16[32,32,128]{2,1,0:T(8,128)(2,1)}), bf16[32,32,128]{2,1,0:T(8,128)(2,1)S(1)}, u32[]{:S(2)}, u32[]{:S(2)}) %all-to-all-start.1) | async-done | bytes 262176 | tf_op jit(solution)/shard_map/exchange_codes/all_to_all | solution.py:357
  46.4 0.0 copy-start.3
  46.4 10.5 %attend.1 = (f32[2048,512]{1,0:T(8,128)S(1)}, f32[8,16,128]{2,1,0:T(8,128)S(1)}) custom-call(bf16[2048,512]{1,0:T(8,128)(2,1)} %queries_hbm.1, bf16[2048,512]{1,0:T(8,128)(2,1)} %copy-done, bf16[128,2048]{1,0:T(8,128)(2,1)S(1)} %get-tuple-element.19.values_t_ref, bf16[32,32,128]{2,1,0:T(8,128)(2,1)S(1)} %all-to-all-done.1.table_ref, ...), custom_call_target="tpu_custom_call" | custom-call | tf_op jit(solution)/shard_map/attend/pallas_call | solution.py:274
  56.8 12.7 %all_to_all.15.squares_ref = f32[8,16,128]{2,1,0:T(8,128)S(1)} all-to-all(f32[8,16,128]{2,1,0:T(8,128)S(1)} %get-tuple-element.24), channel_id=1, replica_groups=mesh['seq'=32,'head'=8] {'head'}, dimensions={0} | all-to-all | bytes 131072 | tf_op jit(solution)/shard_map/exchange_squares/all_to_all | solution.py:363
  69.5 0.0 copy-done.3
  69.5 1.6 %norm.1 = bf16[2048,512]{1,0:T(8,128)(2,1)} custom-call(f32[2048,512]{1,0:T(8,128)S(1)} %get-tuple-element.23.attended_ref, f32[8,16,128]{2,1,0:T(8,128)S(1)} %all_to_all.15.squares_ref, f32[1,512]{1,0:T(1,128)S(1)} %bitcast.2), custom_call_target="tpu_custom_call" | custom-call | tf_op jit(solution)/shard_map/norm/pallas_call | solution.py:365
Async XLA Ops:
  0.0 36.9 %copy-start.1 = (bf16[2048,128]{1,0:T(8,128)(2,1)S(1)}, bf16[2048,128]{1,0:T(8,128)(2,1)}, u32[]{:S(2)}) copy-start(bf16[2048,128]{1,0:T(8,128)(2,1)} %values_ref.1) | copy-start | bytes 1572868
  3.3 24.8 %all-to-all-start = ((bf16[32,56,128]{2,1,0:T(8,128)(2,1)}), bf16[32,56,128]{2,1,0:T(8,128)(2,1)S(1)}, u32[]{:S(2)}, u32[]{:S(2)}) async-start(bf16[32,56,128]{2,1,0:T(8,128)(2,1)} %get-tuple-element.16), calls=%async_computation | async-start | bytes 917504 | tf_op jit(solution)/shard_map/exchange_sums/all_to_all | solution.py:341
  28.9 17.5 %all-to-all-start.1 = ((bf16[32,32,128]{2,1,0:T(8,128)(2,1)}), bf16[32,32,128]{2,1,0:T(8,128)(2,1)S(1)}, u32[]{:S(2)}, u32[]{:S(2)}) async-start(bf16[32,32,128]{2,1,0:T(8,128)(2,1)} %get-tuple-element.20), calls=%async_computation.1 | async-start | bytes 524288 | tf_op jit(solution)/shard_map/exchange_codes/all_to_all | solution.py:357
  37.7 1.3 %copy-start = (bf16[2048,512]{1,0:T(8,128)(2,1)}, bf16[2048,512]{1,0:T(8,128)(2,1)S(1)}, u32[]{:S(2)}) copy-start(bf16[2048,512]{1,0:T(8,128)(2,1)S(1)} %get-tuple-element.18.rows_hbm) | copy-start | bytes 6291460
  39.0 0.6 copy-start.2
  46.4 23.2 %copy-start.3 = (f32[512]{0:T(512)S(1)}, f32[512]{0:T(512)}, u32[]{:S(2)}) copy-start(f32[512]{0:T(512)} %param.9) | copy-start | bytes 6148

commit v7 on v6

--- a/solution.py
+++ b/solution.py
@@ -252,8 +252,10 @@
         for k in range(0, width, DH):
             cols = slice(k, k + DH)
             out[rows, cols] = (attended_ref[rows, cols] * column * gain_ref[:, cols]).astype(BF16)
-        copies.append(pltpu.make_async_copy(out.at[rows], out_hbm.at[rows], ready.at[i]))
-        copies[i].start()
+        if i % 4 == 3:
+            done = slice((i - 3) * CHUNK, (i + 1) * CHUNK)
+            copies.append(pltpu.make_async_copy(out.at[done], out_hbm.at[done], ready.at[i // 4]))
+            copies[-1].start()
     for copy in copies:
         copy.wait()
 
@@ -368,7 +370,7 @@
             out_shape=shape((tokens, width), BF16),
             scratch_shapes=[
                 pltpu.VMEM((tokens, width), BF16),
-                pltpu.SemaphoreType.DMA((chunks,)),
+                pltpu.SemaphoreType.DMA((chunks // 4,)),
             ],
             compiler_params=pltpu.CompilerParams(vmem_limit_bytes=12 * 2**20),
         )(attended, squares, norm_gain.reshape(1, width))

time: 71.6 us -> 71.6 us (level)
  no operation moved by 1% of the time
where the time goes in v7:
time: 71.6 us; the launch traced here: 71.3 us
  starting transfers between devices  19.8 us (28%)
  waiting for transfers between devices  19.7 us (28%)
  Pallas kernels  16.9 us (24%)
  blocking collectives  12.7 us (18%)
  local copies, waits for them, and re-layouts  1.92 us (3%)
    all_to_all x1, waiting for transfers between devices, local(): parts = lax.all_to_all(parts, 'seq', 0, 0)  12.9 us
    all_to_all x1, blocking collectives, local(): squares = lax.all_to_all(squares, 'head', 0, 0)  12.7 us
    all_to_all x1, starting transfers between devices, local(): parts = lax.all_to_all(parts, 'seq', 0, 0)  11.9 us
    pallas_call x1, Pallas kernels, attend(): pl.pallas_call(attend_kernel, out_shape=(shape((tokens, width), F32), sha...  10.5 us
    all_to_all x1, starting transfers between devices, local(): table = lax.all_to_all(table, 'seq', 0, 0)  7.96 us
    all_to_all x1, waiting for transfers between devices, local(): table = lax.all_to_all(table, 'seq', 0, 0)  6.75 us
    pallas_call x1, Pallas kernels, local(): pl.pallas_call(functools.partial(sums_kernel, peers), in_specs=[pl.BlockS...  3.24 us
    unnamed x8, local copies, waits for them, and re-layouts  1.92 us
  transfers between devices with their start and end apart: 2, of which 2 were waited for; matrix products, arithmetic and copies ran while one was open for 0% of the time, Pallas kernels for 1%

profile of v7, /device:TPU:1, one launch (start us, length us, event | category | flops | bytes accessed | tf_op | source)
XLA Modules:
  0.0 71.3 jit_solution(9583702857337845309)
XLA Ops:
  0.0 0.0 copy-start.1
  0.0 3.2 %code_sums.1 = (bf16[32,56,128]{2,1,0:T(8,128)(2,1)}, bf16[512,2048]{1,0:T(8,128)(2,1)S(1)}) custom-call(s32[1,2048]{1,0:T(1,128)} %picks_hbm.1, bf16[2048,128]{1,0:T(8,128)(2,1)} %keys_hbm.1, bf16[2048,128]{1,0:T(8,128)(2,1)} %values_ref.1), custom_call_target="tpu_custom_call" | custom-call | tf_op jit(solution)/shard_map/code_sums/pallas_call | solution.py:328
  3.3 11.9 %all-to-all-start = ((bf16[32,56,128]{2,1,0:T(8,128)(2,1)}), bf16[32,56,128]{2,1,0:T(8,128)(2,1)S(1)}, u32[]{:S(2)}, u32[]{:S(2)}) async-start(bf16[32,56,128]{2,1,0:T(8,128)(2,1)} %get-tuple-element.16), calls=%async_computation | async-start | bytes 917504 | tf_op jit(solution)/shard_map/exchange_sums/all_to_all | solution.py:343
  15.1 12.9 %all-to-all-done.parts_ref = bf16[32,56,128]{2,1,0:T(8,128)(2,1)S(1)} async-done(((bf16[32,56,128]{2,1,0:T(8,128)(2,1)}), bf16[32,56,128]{2,1,0:T(8,128)(2,1)S(1)}, u32[]{:S(2)}, u32[]{:S(2)}) %all-to-all-start) | async-done | bytes 458784 | tf_op jit(solution)/shard_map/exchange_sums/all_to_all | solution.py:343
  28.0 0.8 %combine.1 = (bf16[32,32,128]{2,1,0:T(8,128)(2,1)}, f32[4,128]{1,0:T(4,128)S(1)}) custom-call(s32[1]{0:T(128)} %bitcast.here_ref, bf16[32,56,128]{2,1,0:T(8,128)(2,1)S(1)} %all-to-all-done.parts_ref), custom_call_target="tpu_custom_call" | custom-call | tf_op jit(solution)/shard_map/combine/pallas_call | solution.py:346
  28.9 8.0 %all-to-all-start.1 = ((bf16[32,32,128]{2,1,0:T(8,128)(2,1)}), bf16[32,32,128]{2,1,0:T(8,128)(2,1)S(1)}, u32[]{:S(2)}, u32[]{:S(2)}) async-start(bf16[32,32,128]{2,1,0:T(8,128)(2,1)} %get-tuple-element.20), calls=%async_computation.1 | async-start | bytes 524288 | tf_op jit(solution)/shard_map/exchange_codes/all_to_all | solution.py:359
  36.9 0.0 copy-done.1
  36.9 0.8 %prepare.1 = (bf16[2048,512]{1,0:T(8,128)(2,1)S(1)}, bf16[128,2048]{1,0:T(8,128)(2,1)S(1)}, bf16[512,128]{1,0:T(8,128)(2,1)S(1)}, f32[16,512]{1,0:T(8,128)S(1)}) custom-call(bf16[512,2048]{1,0:T(8,128)(2,1)S(1)} %get-tuple-element.15.member_ref, bf16[2048,128]{1,0:T(8,128)(2,1)S(1)} %copy-done.1, f32[4,128]{1,0:T(4,128)S(1)} %get-tuple-element.17.base_ref), custom_call_target="tpu_custom_call" | custom-call | flops 536870912 | bytes 8388608 | tf_op jit(solution)/shard_map/prepare/pallas_call | solution.py:304
  37.7 0.0 copy-start
  37.7 1.3 %copy-done = bf16[2048,512]{1,0:T(8,128)(2,1)} copy-done((bf16[2048,512]{1,0:T(8,128)(2,1)}, bf16[2048,512]{1,0:T(8,128)(2,1)S(1)}, u32[]{:S(2)}) %copy-start) | copy-done | bytes 2097176
  39.0 0.0 copy-start.2
  39.0 0.6 copy-done.2
  39.6 6.7 %all-to-all-done.1.table_ref = bf16[32,32,128]{2,1,0:T(8,128)(2,1)S(1)} async-done(((bf16[32,32,128]{2,1,0:T(8,128)(2,1)}), bf16[32,32,128]{2,1,0:T(8,128)(2,1)S(1)}, u32[]{:S(2)}, u32[]{:S(2)}) %all-to-all-start.1) | async-done | bytes 262176 | tf_op jit(solution)/shard_map/exchange_codes/all_to_all | solution.py:359
  46.4 0.0 copy-start.3
  46.4 10.5 %attend.1 = (f32[2048,512]{1,0:T(8,128)S(1)}, f32[8,16,128]{2,1,0:T(8,128)S(1)}) custom-call(bf16[2048,512]{1,0:T(8,128)(2,1)} %queries_hbm.1, bf16[2048,512]{1,0:T(8,128)(2,1)} %copy-done, bf16[128,2048]{1,0:T(8,128)(2,1)S(1)} %get-tuple-element.19.values_t_ref, bf16[32,32,128]{2,1,0:T(8,128)(2,1)S(1)} %all-to-all-done.1.table_ref, ...), custom_call_target="tpu_custom_call" | custom-call | tf_op jit(solution)/shard_map/attend/pallas_call | solution.py:276
  56.8 12.7 %all_to_all.15.squares_ref = f32[8,16,128]{2,1,0:T(8,128)S(1)} all-to-all(f32[8,16,128]{2,1,0:T(8,128)S(1)} %get-tuple-element.24), channel_id=1, replica_groups=mesh['seq'=32,'head'=8] {'head'}, dimensions={0} | all-to-all | bytes 131072 | tf_op jit(solution)/shard_map/exchange_squares/all_to_all | solution.py:365
  69.5 0.0 copy-done.3
  69.5 1.5 %norm.1 = bf16[2048,512]{1,0:T(8,128)(2,1)} custom-call(f32[2048,512]{1,0:T(8,128)S(1)} %get-tuple-element.23.attended_ref, f32[8,16,128]{2,1,0:T(8,128)S(1)} %all_to_all.15.squares_ref, f32[1,512]{1,0:T(1,128)S(1)} %bitcast.2), custom_call_target="tpu_custom_call" | custom-call | tf_op jit(solution)/shard_map/norm/pallas_call | solution.py:367
Async XLA Ops:
  0.0 36.9 %copy-start.1 = (bf16[2048,128]{1,0:T(8,128)(2,1)S(1)}, bf16[2048,128]{1,0:T(8,128)(2,1)}, u32[]{:S(2)}) copy-start(bf16[2048,128]{1,0:T(8,128)(2,1)} %values_ref.1) | copy-start | bytes 1572868
  3.3 24.8 %all-to-all-start = ((bf16[32,56,128]{2,1,0:T(8,128)(2,1)}), bf16[32,56,128]{2,1,0:T(8,128)(2,1)S(1)}, u32[]{:S(2)}, u32[]{:S(2)}) async-start(bf16[32,56,128]{2,1,0:T(8,128)(2,1)} %get-tuple-element.16), calls=%async_computation | async-start | bytes 917504 | tf_op jit(solution)/shard_map/exchange_sums/all_to_all | solution.py:343
  28.9 17.5 %all-to-all-start.1 = ((bf16[32,32,128]{2,1,0:T(8,128)(2,1)}), bf16[32,32,128]{2,1,0:T(8,128)(2,1)S(1)}, u32[]{:S(2)}, u32[]{:S(2)}) async-start(bf16[32,32,128]{2,1,0:T(8,128)(2,1)} %get-tuple-element.20), calls=%async_computation.1 | async-start | bytes 524288 | tf_op jit(solution)/shard_map/exchange_codes/all_to_all | solution.py:359
  37.7 1.3 %copy-start = (bf16[2048,512]{1,0:T(8,128)(2,1)}, bf16[2048,512]{1,0:T(8,128)(2,1)S(1)}, u32[]{:S(2)}) copy-start(bf16[2048,512]{1,0:T(8,128)(2,1)S(1)} %get-tuple-element.18.rows_hbm) | copy-start | bytes 6291460
  39.0 0.6 copy-start.2
  46.4 23.2 %copy-start.3 = (f32[512]{0:T(512)S(1)}, f32[512]{0:T(512)}, u32[]{:S(2)}) copy-start(f32[512]{0:T(512)} %param.9) | copy-start | bytes 6148
